TPU v7x, 32 devices: a whole 2x2x4 slice. The times are simulated.
32 devices in a mesh: gx: 4 (over z), gy: 8 (over y, x, core).
Axes of the slice: x: 2, y: 2, z: 4, core: 2. Of those that a mesh axis runs over, the one named last changes fastest.
Arguments:
- initial_basis: float32 [8, 64, 128, 128], P(None, 'gx', 'gy'), may hold values from 0.1 to 0.5
- labels: int32 [64, 128, 128], P('gx', 'gy'), may hold values from 0 to 15
- class_perm: float32 [16], replicated, may hold values from 0.01 to 100
- support: int32 [64, 128, 128], P('gx', 'gy'), may hold values from 0 to 255
Outputs:
- basis: float32 [8, 64, 128, 128], P(None, 'gx', 'gy')
- coarse: float32 [27, 4, 8, 8], P(None, 'gx', 'gy')
Inputs may be any that keep to these rules, and one draw needn't show every extreme that they name: `support`: bit s of a cell's entry says whether the basis function of its block's corner slot s may be nonzero in that cell.
All inputs are finite; a program needn't handle non-finite values.
Results may differ from a plain program's by a relative error of at most 0.0003.
Values sent between devices are 32-bit elements; how exact they have to be, the bound alone decides.
No kernel may reach another device: no remote copies, remote signals or barrier semaphores. Data moves between devices by JAX's collectives and lax.ppermute only.
A program may use at most 64 MiB of HBM per device.

v0:
```python
import functools

import jax
import jax.numpy as jnp
from jax import lax
from jax.experimental import pallas as pl
from jax.experimental.pallas import tpu as pltpu
from jax.sharding import PartitionSpec as P

CB = 16
NCLASS = 16
DEPTH = 4
PAD = CB + 2 * DEPTH
CELLS = PAD * PAD
LANES = 128
SLOTS = 8
FACE = DEPTH * CB
CORNER = tuple((i, j) for i in range(1, DEPTH) for j in range(1, DEPTH) if i + j <= DEPTH)
MIB = 1 << 20
F32 = jnp.float32

step_share = 2.0 / 3.0
renorm_floor = 0.5

FIELD = (16 + CELLS * SLOTS, LANES)
PLAIN = (16 + CELLS, LANES)
COEF = (7, 16 + CELLS, LANES)
FACE_ROWS = FACE * (SLOTS + 1)
CORNER_ROWS = 112


def in_vmem(*shape):
    return pltpu.VMEM(shape, F32)


def pinned(array):
    return pltpu.with_memory_space_constraint(array, pltpu.VMEM)


def in_hbm(array):
    return pltpu.with_memory_space_constraint(array, pltpu.HBM)


VMEM_SPEC = pl.BlockSpec(memory_space=pltpu.VMEM)
SMEM_SPEC = pl.BlockSpec(memory_space=pltpu.SMEM)
HBM_SPEC = pl.BlockSpec(memory_space=pltpu.HBM)


def lane_iota():
    return lax.broadcasted_iota(jnp.int32, (8, LANES), 1)


def slot_iota():
    return lax.broadcasted_iota(jnp.int32, (8, LANES), 0)


def aligned(row):
    return row if isinstance(row, int) else pl.multiple_of(row, 8)


def column(x, y):
    return 8 + (x + DEPTH) * PAD + y + DEPTH


def field_row(x, y):
    return 8 + ((x + DEPTH) * PAD + y + DEPTH) * SLOTS


def is_even(axis):
    return lax.rem(lax.axis_index(axis), 2) == 0


def look_up(label, table):
    level = [table[c] for c in range(NCLASS)]
    for bit in range(4):
        chosen = (label & (1 << bit)) != 0
        level = [jnp.where(chosen, high, low) for low, high in zip(level[0::2], level[1::2])]
    return level[0]


def slot_bits():
    keep = jnp.int32(255)
    keep = jnp.where(lax.axis_index("gx") == lax.axis_size("gx") - 1, keep & 0x0F, keep)
    keep = jnp.where(lax.axis_index("gy") == lax.axis_size("gy") - 1, keep & 0x33, keep)
    keep = jnp.where(lane_iota() >= LANES - CB, keep & 0x55, keep)
    return keep & (1 << slot_iota())


def first_weights(basis, start, stride, support_row, bits):
    found = jnp.broadcast_to(support_row, (8, LANES)) & bits
    return jnp.where(found != 0, basis[pl.ds(start, SLOTS, stride=stride), :], 0.0)


def x_face_kernel(basis_hbm, labels_hbm, support_hbm, table, out_a, out_b, basis, labels, support, sems):
    copies = []
    for side, start in enumerate((0, CB - DEPTH)):
        there = pl.ds(start, DEPTH)
        copies += [
            pltpu.make_async_copy(basis_hbm.at[:, there], basis.at[side], sems.at[3 * side]),
            pltpu.make_async_copy(labels_hbm.at[there], labels.at[side], sems.at[3 * side + 1]),
            pltpu.make_async_copy(support_hbm.at[there], support.at[side], sems.at[3 * side + 2]),
        ]
    for copy in copies:
        copy.start()
    bits = slot_bits()
    high_first = is_even("gx")
    for copy in copies:
        copy.wait()
    basis = basis.reshape(2 * SLOTS * FACE, LANES)
    labels = labels.reshape(2 * FACE, LANES)
    support = support.reshape(2 * FACE, LANES)
    for out, high in ((out_a, high_first), (out_b, jnp.logical_not(high_first))):
        side = jnp.where(high, 1, 0)
        for tile in range(0, FACE, 8):
            at = pl.ds(pl.multiple_of(side * FACE + tile, 8), 8)
            out[SLOTS * FACE + tile : SLOTS * FACE + tile + 8, :] = look_up(labels[at, :], table)

        def one_x(x, _, out=out, side=side):
            for y in range(CB):
                cell = x * CB + y
                out[pl.ds(pl.multiple_of(cell * SLOTS, 8), SLOTS), :] = first_weights(
                    basis, side * (SLOTS * FACE) + cell, FACE, support[pl.ds(side * FACE + cell, 1), :], bits
                )
            return 0

        lax.fori_loop(0, DEPTH, one_x, 0)


def own_kernel(basis_hbm, labels_hbm, support_hbm, table, field, perm, out_a, out_b, basis, labels, support, sems):
    copies = [
        pltpu.make_async_copy(basis_hbm, basis, sems.at[0]),
        pltpu.make_async_copy(labels_hbm, labels, sems.at[1]),
        pltpu.make_async_copy(support_hbm, support, sems.at[2]),
    ]
    for copy in copies:
        copy.start()
    bits = slot_bits()
    for copy in copies:
        copy.wait()
    basis = basis.reshape(SLOTS * CB * CB, LANES)
    support = support.reshape(CB * CB, LANES)

    def one_x(x, _):
        for tile in (0, 8):
            perm[pl.ds(column(x, tile), 8), :] = look_up(labels[x, tile : tile + 8, :], table)
        for y in range(CB):
            field[pl.ds(aligned(field_row(x, y)), SLOTS), :] = first_weights(
                basis, x * CB + y, CB * CB, support[pl.ds(x * CB + y, 1), :], bits
            )
        return 0

    lax.fori_loop(0, CB, one_x, 0)

    even = is_even("gy")
    for out, high in ((out_a, even), (out_b, jnp.logical_not(even))):
        start = jnp.where(high, CB - DEPTH, 0)

        def one_face_x(x, _, out=out, start=start):
            out[pl.ds(SLOTS * FACE + x * DEPTH, DEPTH), :] = perm[pl.ds(column(x, start), DEPTH), :]
            for y in range(DEPTH):
                into = pl.multiple_of((x * DEPTH + y) * SLOTS, 8)
                out[pl.ds(into, SLOTS), :] = field[pl.ds(aligned(field_row(x, start + y)), SLOTS), :]
            return 0

        lax.fori_loop(0, CB, one_face_x, 0)


def corner_kernel(from_a, from_b, out_a, out_b):
    x_even = is_even("gx")
    y_even = is_even("gy")
    for even in (True, False):

        @pl.when(x_even == even)
        def _(even=even):
            high_x, low_x = (from_a, from_b) if even else (from_b, from_a)
            for out, high in ((out_a, y_even), (out_b, jnp.logical_not(y_even))):
                n = 0
                for source, row in ((low_x, lambda i: DEPTH - i), (high_x, lambda i: i - 1)):
                    for i, j in CORNER:
                        cell = row(i) * CB + jnp.where(high, CB - j, j - 1)
                        out[SLOTS * n : SLOTS * n + SLOTS, :] = source[
                            pl.ds(pl.multiple_of(cell * SLOTS, 8), SLOTS), :
                        ]
                        at = SLOTS * 2 * len(CORNER) + n
                        out[at : at + 1, :] = source[pl.ds(SLOTS * FACE + cell, 1), :]
                        n += 1


def conductance(one, two):
    return 2.0 * one * two / jnp.maximum(one + two, 1e-30)


def fill_coef(perm, coef, xs):
    lane = lane_iota()
    for x in xs:
        for tile in range(3):
            at = aligned(column(x, 8 * tile - DEPTH))
            here = perm[pl.ds(at, 8), :]
            x_up = conductance(here, perm[pl.ds(at + PAD, 8), :])
            x_down = conductance(here, perm[pl.ds(at - PAD, 8), :])
            y_up = conductance(here, perm[pl.ds(at + 1, 8), :])
            y_down = conductance(here, perm[pl.ds(at - 1, 8), :])
            z_up = jnp.where(lane == LANES - 1, 0.0, conductance(here, pltpu.roll(here, LANES - 1, 1)))
            z_down = jnp.where(lane == 0, 0.0, conductance(here, pltpu.roll(here, 1, 1)))
            diag = ((x_up + x_down) + (y_up + y_down)) + (z_up + z_down)
            scale = step_share / jnp.maximum(diag, 1e-30)
            for k, term in enumerate((x_up, x_down, y_up, y_down, z_up, z_down)):
                coef[k, pl.ds(at, 8), :] = term * scale
            coef[6, pl.ds(at, 8), :] = diag


class Stencil:
    def __init__(self, coef):
        self.coef = coef
        slot = slot_iota()
        lane = lane_iota()
        self.x_bit = slot >= 4
        self.y_bit = (slot & 2) != 0
        self.z_bit = (slot & 1) != 0
        self.first = (lane % CB) == 0
        self.last = (lane % CB) == CB - 1

    def turned(self, src, cells):
        out = []
        for x, y in cells:
            at = aligned(field_row(x, y))
            here = src[pl.ds(at, SLOTS), :]
            above = jnp.where(self.z_bit, src[pl.ds(at - 1, SLOTS), :], 0.0)
            below = jnp.where(self.z_bit, 0.0, src[pl.ds(at + 1, SLOTS), :])
            out.append(pltpu.roll(jnp.where(self.first, above, here), LANES - 1, 1))
            out.append(pltpu.roll(jnp.where(self.last, below, here), 1, 1))
        return tuple(out)

    def lateral(self, src, x, y):
        at = aligned(field_row(x, y))
        step = PAD * SLOTS

        def read(offset):
            return src[pl.ds(at + offset, SLOTS), :]

        def crosses(place, where):
            return isinstance(place, int) and place in where

        up, down = (-1, CB - 1), (0, CB)
        x_up = jnp.where(self.x_bit, read(step - 4), 0.0) if crosses(x, up) else read(step)
        x_down = jnp.where(self.x_bit, 0.0, read(4 - step)) if crosses(x, down) else read(-step)
        y_up = jnp.where(self.y_bit, read(SLOTS - 2), 0.0) if crosses(y, up) else read(SLOTS)
        y_down = jnp.where(self.y_bit, 0.0, read(2 - SLOTS)) if crosses(y, down) else read(-SLOTS)
        return x_up, x_down, y_up, y_down

    def inflow(self, src, x, y, z_up, z_down):
        at = column(x, y)
        total = None
        for k, value in enumerate((*self.lateral(src, x, y), z_up, z_down)):
            term = jnp.broadcast_to(self.coef[k, pl.ds(at, 1), :], (8, LANES)) * value
            total = term if total is None else total + term
        return total

    def sweep(self, src, dst, cells, turned, last):
        for n, (x, y) in enumerate(cells):
            at = aligned(field_row(x, y))
            here = src[pl.ds(at, SLOTS), :]
            fresh = here * (1.0 - step_share) + self.inflow(src, x, y, turned[2 * n], turned[2 * n + 1])
            fresh = jnp.where(here > 0.0, fresh, 0.0)
            if last:
                total = fresh + pltpu.roll(fresh, 4, 0)
                total = total + pltpu.roll(total, 2, 0)
                total = total + pltpu.roll(total, 1, 0)
                fresh = fresh * (1.0 / jnp.maximum(total, renorm_floor))
            dst[pl.ds(at, SLOTS), :] = fresh

    def product(self, src, cells, turned, sums):
        sums = list(sums)
        for n, (x, y) in enumerate(cells):
            at = aligned(field_row(x, y))
            here = src[pl.ds(at, SLOTS), :]
            inflow = self.inflow(src, x, y, turned[2 * n], turned[2 * n + 1])
            diag = jnp.broadcast_to(self.coef[6, pl.ds(column(x, y), 1), :], (8, LANES))
            image = diag * (here - inflow * (1.0 / step_share))
            for s in range(SLOTS):
                sums[s] = sums[s] + jnp.broadcast_to(src[pl.ds(at + s, 1), :], (8, LANES)) * image
        return tuple(sums)


def run_stage(coef, field_a, field_b, sums, cells_at, steps_of):
    stencil = Stencil(coef)
    fields = (field_a, field_b)
    for level in (1, 2, 3, 4):
        src, dst = fields[(level - 1) % 2], fields[level % 2]
        if level == 4:
            src = field_b
        steps = steps_of(level)
        if steps is None:
            cells = cells_at(level, None)
            turned = stencil.turned(src, cells)
            if level < 4:
                stencil.sweep(src, dst, cells, turned, level == 3)
            else:
                sums = stencil.product(src, cells, turned, sums)
            continue
        start, stop, stride = steps
        first = stencil.turned(src, cells_at(level, start))
        if level < 4:

            def body(n, turned, level=level, src=src, dst=dst, start=start, stride=stride):
                i = start + n * stride
                after = stencil.turned(src, cells_at(level, i + stride))
                stencil.sweep(src, dst, cells_at(level, i), turned, level == 3)
                return after

            lax.fori_loop(0, (stop - start) // stride, body, first)
        else:

            def body(n, carry, level=level, src=src, start=start, stride=stride):
                turned, so_far = carry
                i = start + n * stride
                after = stencil.turned(src, cells_at(level, i + stride))
                return after, stencil.product(src, cells_at(level, i), turned, so_far)

            _, sums = lax.fori_loop(0, (stop - start) // stride, body, (first, sums))
    return sums


def inner_kernel(field_in, perm, field_a, field_b, coef, acc):
    del field_in

    def some_coef(n, _):
        fill_coef(perm, coef, (1 + 2 * n, 2 + 2 * n))
        return 0

    lax.fori_loop(0, (CB - 2) // 2, some_coef, 0)

    def cells_at(level, i):
        return [(i + u, y) for u in range(2) for y in range(level, CB - level)]

    zero = jnp.zeros((8, LANES), F32)
    sums = run_stage(
        coef, field_a, field_b, (zero,) * SLOTS, cells_at, lambda level: (level, CB - level, 2)
    )
    for s in range(SLOTS):
        acc[8 * s : 8 * s + 8, :] = sums[s]


def strip_kernel(*refs):
    x_a, x_b, y_a, y_b = refs[:4]
    perm, field_a, field_b, coef, acc = refs[9:]

    for even in (True, False):

        @pl.when(is_even("gx") == even)
        def _(even=even):
            high, low = (x_a, x_b) if even else (x_b, x_a)
            for source, start in ((low, -DEPTH), (high, CB)):

                def one_x(x, _, source=source, start=start):
                    for y in range(CB):
                        at = pl.multiple_of((x * CB + y) * SLOTS, 8)
                        field_a[pl.ds(aligned(field_row(start + x, y)), SLOTS), :] = source[pl.ds(at, SLOTS), :]
                    at = pl.multiple_of(SLOTS * FACE + x * CB, 8)
                    perm[pl.ds(column(start + x, 0), CB), :] = source[pl.ds(at, CB), :]
                    return 0

                lax.fori_loop(0, DEPTH, one_x, 0)

        @pl.when(is_even("gy") == even)
        def _(even=even):
            high, low = (y_a, y_b) if even else (y_b, y_a)

            def one_x(x, _):
                for source, start in ((low, -DEPTH), (high, CB)):
                    for y in range(DEPTH):
                        at = pl.multiple_of((x * DEPTH + y) * SLOTS, 8)
                        field_a[pl.ds(aligned(field_row(x, start + y)), SLOTS), :] = source[pl.ds(at, SLOTS), :]
                    perm[pl.ds(column(x, start), DEPTH), :] = source[pl.ds(SLOTS * FACE + x * DEPTH, DEPTH), :]
                return 0

            lax.fori_loop(0, CB, one_x, 0)

    def some_coef(n, _):
        fill_coef(perm, coef, (2 * n + 1 - DEPTH, 2 * n + 2 - DEPTH))
        return 0

    lax.fori_loop(0, (PAD - 2) // 2, some_coef, 0)

    def cells_at(level, i):
        across = list(range(level - DEPTH, level)) + list(range(CB - level, CB - level + DEPTH))
        return [(x, i) for x in across] + [(i, y) for y in across]

    sums = tuple(acc[8 * s : 8 * s + 8, :] for s in range(SLOTS))
    sums = run_stage(coef, field_a, field_b, sums, cells_at, lambda level: (level, CB - level, 1))
    for s in range(SLOTS):
        acc[8 * s : 8 * s + 8, :] = sums[s]


def node_tables():
    node = lax.broadcasted_iota(jnp.int32, (16, LANES), 0)
    lane = lax.broadcasted_iota(jnp.int32, (16, LANES), 1)
    block = lane // CB
    group = jnp.where((node == block) | (node == block + 9), 1.0, 0.0)
    pair = lax.broadcasted_iota(jnp.int32, (128, LANES), 0)
    lane = lax.broadcasted_iota(jnp.int32, (128, LANES), 1)
    one, two = (pair >> 3) & 7, pair & 7
    offset = 13
    for bit, weight in ((2, 9), (1, 3), (0, 1)):
        offset = offset + weight * (((two >> bit) & 1) - ((one >> bit) & 1))
    goes = (lane == 32 * (one >> 1) + offset) & ((one & 1) == (pair >> 6))
    return group, jnp.where(goes, 1.0, 0.0)


def corner_cells(level):
    cells = []
    for x in list(range(level - DEPTH, level)) + list(range(CB - level, CB - level + DEPTH)):
        for y in list(range(level - DEPTH, level)) + list(range(CB - level, CB - level + DEPTH)):
            out_x = max(-x, x - CB + 1, 0)
            out_y = max(-y, y - CB + 1, 0)
            if out_x + out_y <= DEPTH - level:
                cells.append((x, y))
    return cells


def last_kernel(*refs):
    c_a, c_b = refs[:2]
    rows_out, perm, field_a, field_b, coef = refs[7:12]
    acc = refs[6]

    for even in (True, False):

        @pl.when(is_even("gy") == even)
        def _(even=even):
            high, low = (c_a, c_b) if even else (c_b, c_a)
            for source, y_of in ((low, lambda j: -j), (high, lambda j: CB - 1 + j)):
                n = 0
                for x_of in (lambda i: -i, lambda i: CB - 1 + i):
                    for i, j in CORNER:
                        x, y = x_of(i), y_of(j)
                        at = field_row(x, y)
                        field_a[at : at + SLOTS, :] = source[SLOTS * n : SLOTS * n + SLOTS, :]
                        at = SLOTS * 2 * len(CORNER) + n
                        perm[column(x, y) : column(x, y) + 1, :] = source[at : at + 1, :]
                        n += 1

    for x in (-3, -1, CB - 1, CB + 1):
        fill_coef(perm, coef, (x, x + 1))

    sums = tuple(acc[8 * s : 8 * s + 8, :] for s in range(SLOTS))
    sums = run_stage(
        coef, field_a, field_b, sums, lambda level, i: corner_cells(level), lambda level: None
    )
    group, select = node_tables()
    reduced = jnp.concatenate(sums, axis=0)
    dot = functools.partial(
        lax.dot_general, precision=lax.Precision.HIGHEST, preferred_element_type=F32
    )
    per_block = dot(group, reduced, (((1,), (1,)), ((), ())))
    rows_out[...] = dot(per_block[0:8], select[0:64], (((1,), (0,)), ((), ()))) + dot(
        per_block[8:16], select[64:128], (((1,), (0,)), ((), ()))
    )


def basis_kernel(field, out):
    flat = out.reshape(SLOTS * CB * CB, LANES)

    def one_x(x, _):
        for y in range(CB):
            flat[pl.ds(x * CB + y, SLOTS, stride=CB * CB), :] = field[pl.ds(aligned(field_row(x, y)), SLOTS), :]
        return 0

    lax.fori_loop(0, CB, one_x, 0)


def swap_pairs(axis, first):
    count = lax.axis_size(axis)
    pairs = []
    for a in range(first, count - 1, 2):
        pairs += [(a, a + 1), (a + 1, a)]
    return pairs


def swap_both(first, second, axis):
    return (
        lax.ppermute(first, axis, swap_pairs(axis, 0)),
        lax.ppermute(second, axis, swap_pairs(axis, 1)),
    )


def ahead(array, by_x, by_y):
    count_x, count_y = lax.axis_size("gx"), lax.axis_size("gy")
    pairs = [
        (x * count_y + y, (x + by_x) * count_y + y + by_y)
        for x in range(count_x - by_x)
        for y in range(count_y - by_y)
    ]
    return lax.ppermute(array, ("gx", "gy"), pairs)


def params(mib):
    return pltpu.CompilerParams(vmem_limit_bytes=mib * MIB)


def shards(initial_basis, labels, class_perm, support):
    size_x, size_y, size_z = labels.shape
    assert (size_x, size_y, size_z) == (CB, CB, LANES)
    whole = [in_hbm(initial_basis), in_hbm(labels), in_hbm(support)]
    face = in_vmem(FACE_ROWS, LANES)
    x_face_a, x_face_b = pl.pallas_call(
        x_face_kernel,
        out_shape=(face, face),
        in_specs=[HBM_SPEC] * 3 + [SMEM_SPEC],
        out_specs=(VMEM_SPEC,) * 2,
        scratch_shapes=[
            pltpu.VMEM((2, SLOTS, DEPTH, CB, LANES), F32),
            pltpu.VMEM((2, DEPTH, CB, LANES), jnp.int32),
            pltpu.VMEM((2, DEPTH, CB, LANES), jnp.int32),
            pltpu.SemaphoreType.DMA((6,)),
        ],
        compiler_params=params(4),
        name="x_faces",
    )(*whole, class_perm)
    x_a, x_b = swap_both(x_face_a, x_face_b, "gx")
    field, perm, y_face_a, y_face_b = pl.pallas_call(
        own_kernel,
        out_shape=(in_vmem(*FIELD), in_vmem(*PLAIN), face, face),
        in_specs=[HBM_SPEC] * 3 + [SMEM_SPEC],
        out_specs=(VMEM_SPEC,) * 4,
        scratch_shapes=[
            pltpu.VMEM((SLOTS, CB, CB, LANES), F32),
            pltpu.VMEM((CB, CB, LANES), jnp.int32),
            pltpu.VMEM((CB, CB, LANES), jnp.int32),
            pltpu.SemaphoreType.DMA((3,)),
        ],
        compiler_params=params(4),
        name="own_tile",
    )(*whole, class_perm)
    y_a, y_b = swap_both(y_face_a, y_face_b, "gy")
    field_a, field_b, coef, acc = pl.pallas_call(
        inner_kernel,
        out_shape=(in_vmem(*FIELD), in_vmem(*FIELD), in_vmem(*COEF), in_vmem(64, LANES)),
        in_specs=[VMEM_SPEC] * 2,
        out_specs=(VMEM_SPEC,) * 4,
        input_output_aliases={0: 0},
        compiler_params=params(4),
        cost_estimate=pl.CostEstimate(flops=10 * MIB, bytes_accessed=8 * MIB, transcendentals=0),
        name="inner_stage",
    )(pinned(field), pinned(perm))
    corner = in_vmem(CORNER_ROWS, LANES)
    corner_a, corner_b = pl.pallas_call(
        corner_kernel,
        out_shape=(corner, corner),
        in_specs=[VMEM_SPEC] * 2,
        out_specs=(VMEM_SPEC,) * 2,
        compiler_params=params(4),
        name="corners",
    )(pinned(x_a), pinned(x_b))
    c_a, c_b = swap_both(corner_a, corner_b, "gy")
    perm, field_a, field_b, coef, acc = pl.pallas_call(
        strip_kernel,
        out_shape=(in_vmem(*PLAIN), in_vmem(*FIELD), in_vmem(*FIELD), in_vmem(*COEF), in_vmem(64, LANES)),
        in_specs=[VMEM_SPEC] * 9,
        out_specs=(VMEM_SPEC,) * 5,
        input_output_aliases={4: 0, 5: 1, 6: 2, 7: 3, 8: 4},
        compiler_params=params(4),
        cost_estimate=pl.CostEstimate(flops=10 * MIB, bytes_accessed=8 * MIB, transcendentals=0),
        name="strip_stage",
    )(*[pinned(a) for a in (x_a, x_b, y_a, y_b, perm, field_a, field_b, coef, acc)])
    rows, _, _, field_b, _ = pl.pallas_call(
        last_kernel,
        out_shape=(in_vmem(8, LANES), in_vmem(*PLAIN), in_vmem(*FIELD), in_vmem(*FIELD), in_vmem(*COEF)),
        in_specs=[VMEM_SPEC] * 7,
        out_specs=(VMEM_SPEC,) * 5,
        input_output_aliases={2: 1, 3: 2, 4: 3, 5: 4},
        compiler_params=params(4),
        name="corner_stage",
    )(*[pinned(a) for a in (c_a, c_b, perm, field_a, field_b, coef, acc)])
    from_x = ahead(rows, 1, 0)
    from_y = ahead(rows, 0, 1)
    from_xy = ahead(rows, 1, 1)
    basis = pl.pallas_call(
        basis_kernel,
        out_shape=jax.ShapeDtypeStruct((SLOTS, CB, CB, LANES), F32),
        in_specs=[VMEM_SPEC],
        out_specs=VMEM_SPEC,
        compiler_params=params(4),
        cost_estimate=pl.CostEstimate(flops=0, bytes_accessed=2 * MIB, transcendentals=0),
        name="basis_out",
    )(pinned(field_b))
    coarse = (rows[:, 0:27] + from_x[:, 64:91]) + (from_y[:, 32:59] + from_xy[:, 96:123])
    return basis, coarse.T.reshape(27, 1, 1, LANES // CB)


def solution(mesh):
    return jax.shard_map(
        shards,
        mesh=mesh,
        in_specs=(P(None, "gx", "gy", None), P("gx", "gy", None), P(), P("gx", "gy", None)),
        out_specs=(P(None, "gx", "gy", None), P(None, "gx", "gy", None)),
        check_vma=False,
    )
```

profile of v0, /device:TPU:1, one launch (start us, length us, event | category | flops | bytes accessed | tf_op | source)
XLA Modules:
  0.0 47.4 jit_solution(9146888838097201848)
XLA Ops:
  0.6 0.6 %copy-done = f32[16]{0:T(128)S(1)} copy-done((f32[16]{0:T(128)S(1)}, f32[16]{0:T(128)}, u32[]{:S(2)}) %copy-start) | copy-done | bytes 88
  1.3 2.1 %x_faces.1 = (f32[576,128]{1,0:T(8,128)S(1)}, f32[576,128]{1,0:T(8,128)S(1)}) custom-call(f32[8,16,16,128]{3,2,1,0:T(8,128)} %basis_hbm.3, s32[16,16,128]{2,1,0:T(8,128)} %labels_hbm.3, s32[16,16,128]{2,1,0:T(8,128)} %support_hbm.3, f32[16]{0:T(128)S(1)} %copy-done), custom_call_target="tpu_custom_call" | custom-call | tf_op jit(solution)/shard_map/x_faces/pallas_call | solution.py:505
  3.4 2.2 %collective-permute-start = (f32[576,128]{1,0:T(8,128)S(1)}, f32[576,128]{1,0:T(8,128)S(1)}, u32[]{:S(2)}, u32[]{:S(2)}) collective-permute-start(f32[576,128]{1,0:T(8,128)S(1)} %get-tuple-element.21), channel_id=1, source_target_pairs={{0,8},{8,0},{16,24},{24,16},{1,9},{9,1},{17,25},{25,17},{2,10},{10... | collective-permute-start | bytes 884744 | tf_op jit(solution)/shard_map/ppermute | solution.py:481
  5.6 0.7 %collective-permute-start.1 = (f32[576,128]{1,0:T(8,128)S(1)}, f32[576,128]{1,0:T(8,128)S(1)}, u32[]{:S(2)}, u32[]{:S(2)}) collective-permute-start(f32[576,128]{1,0:T(8,128)S(1)} %get-tuple-element.22), channel_id=1, source_target_pairs={{8,16},{16,8},{9,17},{17,9},{10,18},{18,10},{11,19},{19,11},{12,20... | collective-permute-start | bytes 884744 | tf_op jit(solution)/shard_map/ppermute | solution.py:482
  6.3 2.9 %own_tile.1 = (f32[4624,128]{1,0:T(8,128)S(1)}, f32[592,128]{1,0:T(8,128)S(1)}, f32[576,128]{1,0:T(8,128)S(1)}, f32[576,128]{1,0:T(8,128)S(1)}) custom-call(f32[8,16,16,128]{3,2,1,0:T(8,128)} %basis_hbm.3, s32[16,16,128]{2,1,0:T(8,128)} %labels_hbm.3, s32[16,16,128]{2,1,0:T(8,128)} %support_hbm.3, f32[16]{0:T(128)S(1)} %copy-done), custom_call_target="tpu_custom_call" | custom-call | tf_op jit(solution)/shard_map/own_tile/pallas_call | solution.py:520
  9.2 1.0 %collective-permute-start.4 = (f32[576,128]{1,0:T(8,128)S(1)}, f32[576,128]{1,0:T(8,128)S(1)}, u32[]{:S(2)}, u32[]{:S(2)}) collective-permute-start(f32[576,128]{1,0:T(8,128)S(1)} %get-tuple-element.25), channel_id=1, source_target_pairs={{0,1},{1,0},{2,3},{3,2},{4,5},{5,4},{6,7},{7,6},{8,9},{9,8},{10,11... | collective-permute-start | bytes 884744 | tf_op jit(solution)/shard_map/ppermute | solution.py:481
  10.2 3.0 %collective-permute-start.5 = (f32[576,128]{1,0:T(8,128)S(1)}, f32[576,128]{1,0:T(8,128)S(1)}, u32[]{:S(2)}, u32[]{:S(2)}) collective-permute-start(f32[576,128]{1,0:T(8,128)S(1)} %get-tuple-element.26), channel_id=1, source_target_pairs={{1,2},{2,1},{3,4},{4,3},{5,6},{6,5},{9,10},{10,9},{11,12},{12,11},... | collective-permute-start | bytes 884744 | tf_op jit(solution)/shard_map/ppermute | solution.py:482
  13.2 0.0 collective-permute-done.from_a.refs_0_
  13.2 0.0 collective-permute-done.1.from_b.refs_1_
  13.3 0.4 collective-permute-start.2
  13.7 3.2 %collective-permute-start.3 = (f32[112,128]{1,0:T(8,128)S(1)}, f32[112,128]{1,0:T(8,128)S(1)}, u32[]{:S(2)}, u32[]{:S(2)}) collective-permute-start(f32[112,128]{1,0:T(8,128)S(1)} %get-tuple-element.24), channel_id=1, source_target_pairs={{1,2},{2,1},{3,4},{4,3},{5,6},{6,5},{9,10},{10,9},{11,12},{12,11},... | collective-permute-start | bytes 172040 | tf_op jit(solution)/shard_map/ppermute | solution.py:482
  16.9 5.4 %inner_stage.1 = (f32[4624,128]{1,0:T(8,128)S(1)}, f32[4624,128]{1,0:T(8,128)S(1)}, f32[7,592,128]{2,1,0:T(8,128)S(1)}, f32[64,128]{1,0:T(8,128)S(1)}) custom-call(f32[4624,128]{1,0:T(8,128)S(1)} %get-tuple-element.28.field_in, f32[592,128]{1,0:T(8,128)S(1)} %get-tuple-element.27.perm.refs_4_), custom_call_target="tpu_custom_call", output_to_operand_aliasing={{0}: (0, {})} | custom-call | flops 10485760 | bytes 8388608 | tf_op jit(solution)/shard_map/inner_stage/pallas_call | solution.py:535
  22.2 0.0 collective-permute-done.4.refs_2_
  22.3 8.4 %strip_stage.1 = (f32[592,128]{1,0:T(8,128)S(1)}, f32[4624,128]{1,0:T(8,128)S(1)}, f32[4624,128]{1,0:T(8,128)S(1)}, f32[7,592,128]{2,1,0:T(8,128)S(1)}, f32[64,128]{1,0:T(8,128)S(1)}) custom-call(f32[576,128]{1,0:T(8,128)S(1)} %collective-permute-done.from_a.refs_0_, ...), custom_call_target="tpu_custom_call", output_to_operand_aliasing={{0}: (4, {}), {1}: (5, {}), {2}: (6, {}), {3}: (7, {}), {4}... | custom-call | flops 10485760 | bytes 8388608 | tf_op jit(solution)/shard_map/strip_stage/pallas_call | solution.py:555
  30.7 0.0 collective-permute-done.2.refs_0_
  30.7 0.0 collective-permute-done.3.refs_1_
  30.7 1.6 %corner_stage.1 = (f32[8,128]{1,0:T(8,128)S(1)}, f32[592,128]{1,0:T(8,128)S(1)}, f32[4624,128]{1,0:T(8,128)S(1)}, f32[4624,128]{1,0:T(8,128)S(1)}, f32[7,592,128]{2,1,0:T(8,128)S(1)}) custom-call(f32[112,128]{1,0:T(8,128)S(1)} %collective-permute-done.2.refs_0_, ...), custom_call_target="tpu_custom_call", output_to_operand_aliasing={{1}: (2, {}), {2}: (3, {}), {3}: (4, {}), {4}: (5, {})} | custom-call | tf_op jit(solution)/shard_map/corner_stage/pallas_call | solution.py:565
  32.3 6.2 %collective-permute-start.6 = (f32[8,128]{1,0:T(8,128)S(1)}, f32[8,128]{1,0:T(8,128)S(1)}, u32[]{:S(2)}, u32[]{:S(2)}) collective-permute-start(f32[8,128]{1,0:T(8,128)S(1)} %get-tuple-element.39), channel_id=1, source_target_pairs={{0,8},{1,9},{2,10},{3,11},{4,12},{5,13},{6,14},{7,15},{8,16},{9,17... | collective-permute-start | bytes 12296 | tf_op jit(solution)/shard_map/ppermute | solution.py:493
  38.5 2.8 %collective-permute-start.7 = (f32[8,128]{1,0:T(8,128)S(1)}, f32[8,128]{1,0:T(8,128)S(1)}, u32[]{:S(2)}, u32[]{:S(2)}) collective-permute-start(f32[8,128]{1,0:T(8,128)S(1)} %get-tuple-element.39), channel_id=1, source_target_pairs={{0,1},{1,2},{2,3},{3,4},{4,5},{5,6},{6,7},{8,9},{9,10},{10,11},{11... | collective-permute-start | bytes 12296 | tf_op jit(solution)/shard_map/ppermute | solution.py:493
  41.3 3.8 %collective-permute-start.8 = (f32[8,128]{1,0:T(8,128)S(1)}, f32[8,128]{1,0:T(8,128)S(1)}, u32[]{:S(2)}, u32[]{:S(2)}) collective-permute-start(f32[8,128]{1,0:T(8,128)S(1)} %get-tuple-element.39), channel_id=1, source_target_pairs={{0,9},{1,10},{2,11},{3,12},{4,13},{5,14},{6,15},{8,17},{9,18},{10,... | collective-permute-start | bytes 12296 | tf_op jit(solution)/shard_map/ppermute | solution.py:493
  45.1 1.6 %basis_out.1 = f32[8,16,16,128]{3,2,1,0:T(8,128)} custom-call(f32[4624,128]{1,0:T(8,128)S(1)} %get-tuple-element.38.field), custom_call_target="tpu_custom_call" | custom-call | bytes 2097152 | tf_op jit(solution)/shard_map/basis_out/pallas_call | solution.py:577
  46.7 0.0 collective-permute-done.6
  46.7 0.0 collective-permute-done.7
  46.7 0.7 %add_bitcast_fusion = f32[27,1,1,8]{0,3,2,1:T(8,128)} fusion(f32[8,128]{1,0:T(8,128)S(1)} %collective-permute-done.8, f32[8,128]{1,0:T(8,128)S(1)} %collective-permute-done.7, f32[8,128]{1,0:T(8,128)S(1)} %collective-permute-done.6, f32[8,128]{1,0:T(8,128)S(1)} %get-tuple-element.39), kind=kLoop, calls=%fused_computation | loop fusion | flops 648 | bytes 4320 | tf_op jit(solution)/shard_map/reshape | solution.py:587
  (4 shorter events, 0.0 us)
Async XLA Ops:
  0.6 0.7 %copy-start = (f32[16]{0:T(128)S(1)}, f32[16]{0:T(128)}, u32[]{:S(2)}) copy-start(f32[16]{0:T(128)} %table.3) | copy-start | bytes 196
  3.4 9.8 %collective-permute-start = (f32[576,128]{1,0:T(8,128)S(1)}, f32[576,128]{1,0:T(8,128)S(1)}, u32[]{:S(2)}, u32[]{:S(2)}) collective-permute-start(f32[576,128]{1,0:T(8,128)S(1)} %get-tuple-element.21), channel_id=1, source_target_pairs={{0,8},{8,0},{16,24},{24,16},{1,9},{9,1},{17,25},{25,17},{2,10},{10... | collective-permute-start | bytes 884744 | tf_op jit(solution)/shard_map/ppermute | solution.py:481
  5.6 7.6 %collective-permute-start.1 = (f32[576,128]{1,0:T(8,128)S(1)}, f32[576,128]{1,0:T(8,128)S(1)}, u32[]{:S(2)}, u32[]{:S(2)}) collective-permute-start(f32[576,128]{1,0:T(8,128)S(1)} %get-tuple-element.22), channel_id=1, source_target_pairs={{8,16},{16,8},{9,17},{17,9},{10,18},{18,10},{11,19},{19,11},{12,20... | collective-permute-start | bytes 884744 | tf_op jit(solution)/shard_map/ppermute | solution.py:482
  9.2 13.1 %collective-permute-start.4 = (f32[576,128]{1,0:T(8,128)S(1)}, f32[576,128]{1,0:T(8,128)S(1)}, u32[]{:S(2)}, u32[]{:S(2)}) collective-permute-start(f32[576,128]{1,0:T(8,128)S(1)} %get-tuple-element.25), channel_id=1, source_target_pairs={{0,1},{1,0},{2,3},{3,2},{4,5},{5,4},{6,7},{7,6},{8,9},{9,8},{10,11... | collective-permute-start | bytes 884744 | tf_op jit(solution)/shard_map/ppermute | solution.py:481
  10.2 12.0 %collective-permute-start.5 = (f32[576,128]{1,0:T(8,128)S(1)}, f32[576,128]{1,0:T(8,128)S(1)}, u32[]{:S(2)}, u32[]{:S(2)}) collective-permute-start(f32[576,128]{1,0:T(8,128)S(1)} %get-tuple-element.26), channel_id=1, source_target_pairs={{1,2},{2,1},{3,4},{4,3},{5,6},{6,5},{9,10},{10,9},{11,12},{12,11},... | collective-permute-start | bytes 884744 | tf_op jit(solution)/shard_map/ppermute | solution.py:482
  13.3 17.4 %collective-permute-start.2 = (f32[112,128]{1,0:T(8,128)S(1)}, f32[112,128]{1,0:T(8,128)S(1)}, u32[]{:S(2)}, u32[]{:S(2)}) collective-permute-start(f32[112,128]{1,0:T(8,128)S(1)} %get-tuple-element.23), channel_id=1, source_target_pairs={{0,1},{1,0},{2,3},{3,2},{4,5},{5,4},{6,7},{7,6},{8,9},{9,8},{10,11... | collective-permute-start | bytes 172040 | tf_op jit(solution)/shard_map/ppermute | solution.py:481
  13.7 17.0 %collective-permute-start.3 = (f32[112,128]{1,0:T(8,128)S(1)}, f32[112,128]{1,0:T(8,128)S(1)}, u32[]{:S(2)}, u32[]{:S(2)}) collective-permute-start(f32[112,128]{1,0:T(8,128)S(1)} %get-tuple-element.24), channel_id=1, source_target_pairs={{1,2},{2,1},{3,4},{4,3},{5,6},{6,5},{9,10},{10,9},{11,12},{12,11},... | collective-permute-start | bytes 172040 | tf_op jit(solution)/shard_map/ppermute | solution.py:482
  32.3 14.4 %collective-permute-start.6 = (f32[8,128]{1,0:T(8,128)S(1)}, f32[8,128]{1,0:T(8,128)S(1)}, u32[]{:S(2)}, u32[]{:S(2)}) collective-permute-start(f32[8,128]{1,0:T(8,128)S(1)} %get-tuple-element.39), channel_id=1, source_target_pairs={{0,8},{1,9},{2,10},{3,11},{4,12},{5,13},{6,14},{7,15},{8,16},{9,17... | collective-permute-start | bytes 12296 | tf_op jit(solution)/shard_map/ppermute | solution.py:493
  38.5 8.2 %collective-permute-start.7 = (f32[8,128]{1,0:T(8,128)S(1)}, f32[8,128]{1,0:T(8,128)S(1)}, u32[]{:S(2)}, u32[]{:S(2)}) collective-permute-start(f32[8,128]{1,0:T(8,128)S(1)} %get-tuple-element.39), channel_id=1, source_target_pairs={{0,1},{1,2},{2,3},{3,4},{4,5},{5,6},{6,7},{8,9},{9,10},{10,11},{11... | collective-permute-start | bytes 12296 | tf_op jit(solution)/shard_map/ppermute | solution.py:493
  41.3 5.4 %collective-permute-start.8 = (f32[8,128]{1,0:T(8,128)S(1)}, f32[8,128]{1,0:T(8,128)S(1)}, u32[]{:S(2)}, u32[]{:S(2)}) collective-permute-start(f32[8,128]{1,0:T(8,128)S(1)} %get-tuple-element.39), channel_id=1, source_target_pairs={{0,9},{1,10},{2,11},{3,12},{4,13},{5,14},{6,15},{8,17},{9,18},{10,... | collective-permute-start | bytes 12296 | tf_op jit(solution)/shard_map/ppermute | solution.py:493
where the time goes:
time: 47.7 us; the launch traced here: 47.4 us
  starting transfers between devices  23.2 us (49%)
  Pallas kernels  22 us (46%)
  between operations  0.8 us (2%)
  other arithmetic  0.67 us (1%)
  local copies, waits for them, and re-layouts  0.65 us (1%)
    ppermute x3, starting transfers between devices, ahead(): return lax.ppermute(array, ('gx', 'gy'), pairs)  12.8 us
    pallas_call x1, Pallas kernels, shards(): pl.pallas_call(strip_kernel, out_shape=(in_vmem(*PLAIN), in_vmem(*FIELD),...  8.4 us
    ppermute x3, starting transfers between devices, swap_both(): lax.ppermute(second, axis, swap_pairs(axis, 1))  6.9 us
    pallas_call x1, Pallas kernels, shards(): pl.pallas_call(inner_kernel, out_shape=(in_vmem(*FIELD), in_vmem(*FIELD),...  5.35 us
    ppermute x3, starting transfers between devices, swap_both(): lax.ppermute(first, axis, swap_pairs(axis, 0))  3.57 us
    pallas_call x1, Pallas kernels, shards(): pl.pallas_call(own_kernel, out_shape=(in_vmem(*FIELD), in_vmem(*PLAIN), f...  2.91 us
    pallas_call x1, Pallas kernels, shards(): pl.pallas_call(x_face_kernel, out_shape=(face, face), in_specs=[HBM_SPEC]...  2.11 us
    pallas_call x1, Pallas kernels, shards(): pl.pallas_call(basis_kernel, out_shape=jax.ShapeDtypeStruct((SLOTS, CB, C...  1.62 us
  transfers between devices with their start and end apart: 9, of which 0 were waited for; matrix products, arithmetic and copies ran while one was open for 0% of the time, Pallas kernels for 39%

commit v1 on v0

--- a/solution.py
+++ b/solution.py
@@ -91,81 +91,76 @@
     return jnp.where(found != 0, basis[pl.ds(start, SLOTS, stride=stride), :], 0.0)
 
 
-def x_face_kernel(basis_hbm, labels_hbm, support_hbm, table, out_a, out_b, basis, labels, support, sems):
-    copies = []
-    for side, start in enumerate((0, CB - DEPTH)):
-        there = pl.ds(start, DEPTH)
-        copies += [
-            pltpu.make_async_copy(basis_hbm.at[:, there], basis.at[side], sems.at[3 * side]),
-            pltpu.make_async_copy(labels_hbm.at[there], labels.at[side], sems.at[3 * side + 1]),
-            pltpu.make_async_copy(support_hbm.at[there], support.at[side], sems.at[3 * side + 2]),
-        ]
-    for copy in copies:
+def own_kernel(
+    basis_hbm, labels_hbm, support_hbm, table_hbm, field, perm, x_a, x_b, y_a, y_b, basis, labels, support, table, sems
+):
+    fetch_table = pltpu.make_async_copy(table_hbm, table, sems.at[0])
+    fetch_labels = pltpu.make_async_copy(labels_hbm, labels, sems.at[1])
+    fetch_support = pltpu.make_async_copy(support_hbm, support, sems.at[2])
+    fetch_basis = [
+        pltpu.make_async_copy(basis_hbm.at[:, pl.ds(DEPTH * part, DEPTH)], basis.at[part], sems.at[3 + part])
+        for part in range(CB // DEPTH)
+    ]
+    for copy in (fetch_table, fetch_labels, fetch_support, *fetch_basis):
         copy.start()
     bits = slot_bits()
-    high_first = is_even("gx")
-    for copy in copies:
-        copy.wait()
-    basis = basis.reshape(2 * SLOTS * FACE, LANES)
-    labels = labels.reshape(2 * FACE, LANES)
-    support = support.reshape(2 * FACE, LANES)
-    for out, high in ((out_a, high_first), (out_b, jnp.logical_not(high_first))):
-        side = jnp.where(high, 1, 0)
-        for tile in range(0, FACE, 8):
-            at = pl.ds(pl.multiple_of(side * FACE + tile, 8), 8)
-            out[SLOTS * FACE + tile : SLOTS * FACE + tile + 8, :] = look_up(labels[at, :], table)
-
-        def one_x(x, _, out=out, side=side):
-            for y in range(CB):
-                cell = x * CB + y
-                out[pl.ds(pl.multiple_of(cell * SLOTS, 8), SLOTS), :] = first_weights(
-                    basis, side * (SLOTS * FACE) + cell, FACE, support[pl.ds(side * FACE + cell, 1), :], bits
-                )
-            return 0
-
-        lax.fori_loop(0, DEPTH, one_x, 0)
-
-
-def own_kernel(basis_hbm, labels_hbm, support_hbm, table, field, perm, out_a, out_b, basis, labels, support, sems):
-    copies = [
-        pltpu.make_async_copy(basis_hbm, basis, sems.at[0]),
-        pltpu.make_async_copy(labels_hbm, labels, sems.at[1]),
-        pltpu.make_async_copy(support_hbm, support, sems.at[2]),
-    ]
-    for copy in copies:
-        copy.start()
-    bits = slot_bits()
-    for copy in copies:
+    fetch_table.wait()
+    fetch_labels.wait()
+
+    def one_perm(x, _):
+        for tile in (0, 8):
+            perm[pl.ds(column(x, tile), 8), :] = look_up(labels[x, tile : tile + 8, :], table)
+        return 0
+
+    lax.fori_loop(0, CB, one_perm, 0, unroll=4)
+    fetch_support.wait()
+    for copy in fetch_basis:
         copy.wait()
     basis = basis.reshape(SLOTS * CB * CB, LANES)
     support = support.reshape(CB * CB, LANES)
 
     def one_x(x, _):
-        for tile in (0, 8):
-            perm[pl.ds(column(x, tile), 8), :] = look_up(labels[x, tile : tile + 8, :], table)
         for y in range(CB):
+            start = (x // DEPTH) * (SLOTS * FACE) + (x % DEPTH) * CB + y
             field[pl.ds(aligned(field_row(x, y)), SLOTS), :] = first_weights(
-                basis, x * CB + y, CB * CB, support[pl.ds(x * CB + y, 1), :], bits
+                basis, start, FACE, support[pl.ds(x * CB + y, 1), :], bits
             )
         return 0
 
-    lax.fori_loop(0, CB, one_x, 0)
-
-    even = is_even("gy")
-    for out, high in ((out_a, even), (out_b, jnp.logical_not(even))):
-        start = jnp.where(high, CB - DEPTH, 0)
-
-        def one_face_x(x, _, out=out, start=start):
-            out[pl.ds(SLOTS * FACE + x * DEPTH, DEPTH), :] = perm[pl.ds(column(x, start), DEPTH), :]
-            for y in range(DEPTH):
-                into = pl.multiple_of((x * DEPTH + y) * SLOTS, 8)
-                out[pl.ds(into, SLOTS), :] = field[pl.ds(aligned(field_row(x, start + y)), SLOTS), :]
-            return 0
-
-        lax.fori_loop(0, CB, one_face_x, 0)
-
-
-def corner_kernel(from_a, from_b, out_a, out_b):
+    lax.fori_loop(0, CB, one_x, 0, unroll=2)
+
+    def x_face(out, start):
+        out[SLOTS * FACE : FACE_ROWS, :] = jnp.concatenate(
+            [perm[column(start + x, 0) : column(start + x, 0) + CB, :] for x in range(DEPTH)], axis=0
+        )
+        for x in range(DEPTH):
+            rows = CB * SLOTS
+            out[x * rows : (x + 1) * rows, :] = field[field_row(start + x, 0) : field_row(start + x, CB), :]
+
+    def y_face(out, start):
+        rows = DEPTH * SLOTS
+        for x in range(CB):
+            at = SLOTS * FACE + x * DEPTH
+            out[at : at + DEPTH, :] = perm[column(x, start) : column(x, start + DEPTH), :]
+            out[x * rows : (x + 1) * rows, :] = field[field_row(x, start) : field_row(x, start + DEPTH), :]
+
+    for even in (True, False):
+
+        @pl.when(is_even("gx") == even)
+        def _(even=even):
+            high, low = (x_a, x_b) if even else (x_b, x_a)
+            x_face(low, 0)
+            x_face(high, CB - DEPTH)
+
+        @pl.when(is_even("gy") == even)
+        def _(even=even):
+            high, low = (y_a, y_b) if even else (y_b, y_a)
+            y_face(low, 0)
+            y_face(high, CB - DEPTH)
+
+
+def corner_kernel(from_a, from_b, inner_done, out_a, out_b):
+    del inner_done
     x_even = is_even("gx")
     y_even = is_even("gy")
     for even in (True, False):
@@ -290,34 +285,20 @@
         if level == 4:
             src = field_b
         steps = steps_of(level)
-        if steps is None:
-            cells = cells_at(level, None)
+
+        def one_step(i, sums, level=level, src=src, dst=dst):
+            cells = cells_at(level, i)
             turned = stencil.turned(src, cells)
             if level < 4:
                 stencil.sweep(src, dst, cells, turned, level == 3)
-            else:
-                sums = stencil.product(src, cells, turned, sums)
-            continue
-        start, stop, stride = steps
-        first = stencil.turned(src, cells_at(level, start))
-        if level < 4:
-
-            def body(n, turned, level=level, src=src, dst=dst, start=start, stride=stride):
-                i = start + n * stride
-                after = stencil.turned(src, cells_at(level, i + stride))
-                stencil.sweep(src, dst, cells_at(level, i), turned, level == 3)
-                return after
-
-            lax.fori_loop(0, (stop - start) // stride, body, first)
+                return sums
+            return stencil.product(src, cells, turned, sums)
+
+        if steps is None:
+            sums = one_step(None, sums)
         else:
-
-            def body(n, carry, level=level, src=src, start=start, stride=stride):
-                turned, so_far = carry
-                i = start + n * stride
-                after = stencil.turned(src, cells_at(level, i + stride))
-                return after, stencil.product(src, cells_at(level, i), turned, so_far)
-
-            _, sums = lax.fori_loop(0, (stop - start) // stride, body, (first, sums))
+            start, count, stride = steps
+            sums = lax.fori_loop(0, count, lambda n, c, s=start, d=stride, f=one_step: f(s + n * d, c), sums)
     return sums
 
 
@@ -325,17 +306,17 @@
     del field_in
 
     def some_coef(n, _):
-        fill_coef(perm, coef, (1 + 2 * n, 2 + 2 * n))
+        fill_coef(perm, coef, [1 + 7 * n + u for u in range(7)])
         return 0
 
-    lax.fori_loop(0, (CB - 2) // 2, some_coef, 0)
+    lax.fori_loop(0, 2, some_coef, 0)
 
     def cells_at(level, i):
-        return [(i + u, y) for u in range(2) for y in range(level, CB - level)]
+        return [(i + u, y) for u in range(CB // 2 - level) for y in range(level, CB - level)]
 
     zero = jnp.zeros((8, LANES), F32)
     sums = run_stage(
-        coef, field_a, field_b, (zero,) * SLOTS, cells_at, lambda level: (level, CB - level, 2)
+        coef, field_a, field_b, (zero,) * SLOTS, cells_at, lambda level: (level, 2, CB // 2 - level)
     )
     for s in range(SLOTS):
         acc[8 * s : 8 * s + 8, :] = sums[s]
@@ -377,17 +358,17 @@
             lax.fori_loop(0, CB, one_x, 0)
 
     def some_coef(n, _):
-        fill_coef(perm, coef, (2 * n + 1 - DEPTH, 2 * n + 2 - DEPTH))
+        fill_coef(perm, coef, [11 * n + 1 - DEPTH + u for u in range(11)])
         return 0
 
-    lax.fori_loop(0, (PAD - 2) // 2, some_coef, 0)
+    lax.fori_loop(0, 2, some_coef, 0)
 
     def cells_at(level, i):
         across = list(range(level - DEPTH, level)) + list(range(CB - level, CB - level + DEPTH))
-        return [(x, i) for x in across] + [(i, y) for y in across]
+        return [c for u in range(CB // 2 - level) for c in [(x, i + u) for x in across] + [(i + u, y) for y in across]]
 
     sums = tuple(acc[8 * s : 8 * s + 8, :] for s in range(SLOTS))
-    sums = run_stage(coef, field_a, field_b, sums, cells_at, lambda level: (level, CB - level, 1))
+    sums = run_stage(coef, field_a, field_b, sums, cells_at, lambda level: (level, 2, CB // 2 - level))
     for s in range(SLOTS):
         acc[8 * s : 8 * s + 8, :] = sums[s]
 
@@ -500,37 +481,23 @@
 def shards(initial_basis, labels, class_perm, support):
     size_x, size_y, size_z = labels.shape
     assert (size_x, size_y, size_z) == (CB, CB, LANES)
-    whole = [in_hbm(initial_basis), in_hbm(labels), in_hbm(support)]
     face = in_vmem(FACE_ROWS, LANES)
-    x_face_a, x_face_b = pl.pallas_call(
-        x_face_kernel,
-        out_shape=(face, face),
-        in_specs=[HBM_SPEC] * 3 + [SMEM_SPEC],
-        out_specs=(VMEM_SPEC,) * 2,
+    field, perm, x_face_a, x_face_b, y_face_a, y_face_b = pl.pallas_call(
+        own_kernel,
+        out_shape=(in_vmem(*FIELD), in_vmem(*PLAIN), face, face, face, face),
+        in_specs=[HBM_SPEC] * 4,
+        out_specs=(VMEM_SPEC,) * 6,
         scratch_shapes=[
-            pltpu.VMEM((2, SLOTS, DEPTH, CB, LANES), F32),
-            pltpu.VMEM((2, DEPTH, CB, LANES), jnp.int32),
-            pltpu.VMEM((2, DEPTH, CB, LANES), jnp.int32),
-            pltpu.SemaphoreType.DMA((6,)),
-        ],
-        compiler_params=params(4),
-        name="x_faces",
-    )(*whole, class_perm)
-    x_a, x_b = swap_both(x_face_a, x_face_b, "gx")
-    field, perm, y_face_a, y_face_b = pl.pallas_call(
-        own_kernel,
-        out_shape=(in_vmem(*FIELD), in_vmem(*PLAIN), face, face),
-        in_specs=[HBM_SPEC] * 3 + [SMEM_SPEC],
-        out_specs=(VMEM_SPEC,) * 4,
-        scratch_shapes=[
-            pltpu.VMEM((SLOTS, CB, CB, LANES), F32),
+            pltpu.VMEM((CB // DEPTH, SLOTS, DEPTH, CB, LANES), F32),
             pltpu.VMEM((CB, CB, LANES), jnp.int32),
             pltpu.VMEM((CB, CB, LANES), jnp.int32),
-            pltpu.SemaphoreType.DMA((3,)),
+            pltpu.SMEM((NCLASS,), F32),
+            pltpu.SemaphoreType.DMA((3 + CB // DEPTH,)),
         ],
         compiler_params=params(4),
         name="own_tile",
-    )(*whole, class_perm)
+    )(*[in_hbm(a) for a in (initial_basis, labels, support, class_perm)])
+    x_a, x_b = swap_both(x_face_a, x_face_b, "gx")
     y_a, y_b = swap_both(y_face_a, y_face_b, "gy")
     field_a, field_b, coef, acc = pl.pallas_call(
         inner_kernel,
@@ -546,11 +513,11 @@
     corner_a, corner_b = pl.pallas_call(
         corner_kernel,
         out_shape=(corner, corner),
-        in_specs=[VMEM_SPEC] * 2,
+        in_specs=[VMEM_SPEC] * 3,
         out_specs=(VMEM_SPEC,) * 2,
         compiler_params=params(4),
         name="corners",
-    )(pinned(x_a), pinned(x_b))
+    )(pinned(x_a), pinned(x_b), pinned(acc))
     c_a, c_b = swap_both(corner_a, corner_b, "gy")
     perm, field_a, field_b, coef, acc = pl.pallas_call(
         strip_kernel,

time: 47.7 us -> 37.4 us (0.78)
  Pallas kernels: 22 us -> 11.9 us
  waiting for transfers between devices: 0.03 us -> 1.35 us
  starting transfers between devices: 23.2 us -> 22.5 us
  local copies, waits for them, and re-layouts: 0.65 us -> 0 us
    pallas_call x1, Pallas kernels: 8.4 us -> 3.87 us  [shards(): pl.pallas_call(strip_kernel, out_shape=(in_vmem(*PLAIN), in_vmem(*FIELD),...]
    pallas_call x1, Pallas kernels: 5.35 us -> 2.56 us  [shards(): pl.pallas_call(inner_kernel, out_shape=(in_vmem(*FIELD), in_vmem(*FIELD),...]
    pallas_call x1 -> x0, Pallas kernels: 2.11 us -> none  [shards(): pl.pallas_call(x_face_kernel, out_shape=(face, face), in_specs=[HBM_SPEC]...]
    ppermute x3, waiting for transfers between devices: 0.01 us -> 1.33 us  [swap_both(): lax.ppermute(second, axis, swap_pairs(axis, 1))]
    ppermute x3, starting transfers between devices: 12.8 us -> 11.7 us  [ahead(): return lax.ppermute(array, ('gx', 'gy'), pairs)]
    pallas_call x1, Pallas kernels: 2.91 us -> 2.25 us  [shards(): pl.pallas_call(own_kernel, out_shape=(in_vmem(*FIELD), in_vmem(*PLAIN), f...]
    unnamed x2 -> x0, local copies, waits for them, and re-layouts: 0.65 us -> none
  transfers between devices with their start and end apart: 9 -> 9, of which waited for: 0 -> 1; matrix products, arithmetic and copies ran while one was open for 0% -> 0% of each run, Pallas kernels for 39% -> 22%
where the time goes in v1:
time: 37.4 us; the launch traced here: 37.1 us
  starting transfers between devices  22.5 us (60%)
  Pallas kernels  11.9 us (32%)
  waiting for transfers between devices  1.35 us (4%)
  between operations  0.76 us (2%)
  other arithmetic  0.67 us (2%)
    ppermute x3, starting transfers between devices, ahead(): return lax.ppermute(array, ('gx', 'gy'), pairs)  11.7 us
    ppermute x3, starting transfers between devices, swap_both(): lax.ppermute(second, axis, swap_pairs(axis, 1))  6.87 us
    ppermute x3, starting transfers between devices, swap_both(): lax.ppermute(first, axis, swap_pairs(axis, 0))  3.92 us
    pallas_call x1, Pallas kernels, shards(): pl.pallas_call(strip_kernel, out_shape=(in_vmem(*PLAIN), in_vmem(*FIELD),...  3.87 us
    pallas_call x1, Pallas kernels, shards(): pl.pallas_call(inner_kernel, out_shape=(in_vmem(*FIELD), in_vmem(*FIELD),...  2.56 us
    pallas_call x1, Pallas kernels, shards(): pl.pallas_call(own_kernel, out_shape=(in_vmem(*FIELD), in_vmem(*PLAIN), f...  2.25 us
    pallas_call x1, Pallas kernels, shards(): pl.pallas_call(basis_kernel, out_shape=jax.ShapeDtypeStruct((SLOTS, CB, C...  1.62 us
    pallas_call x1, Pallas kernels, shards(): pl.pallas_call(last_kernel, out_shape=(in_vmem(8, LANES), in_vmem(*PLAIN)...  1.56 us
  transfers between devices with their start and end apart: 9, of which 1 were waited for; matrix products, arithmetic and copies ran while one was open for 0% of the time, Pallas kernels for 22%

profile of v1, /device:TPU:1, one launch (start us, length us, event | category | flops | bytes accessed | tf_op | source)
XLA Modules:
  0.0 37.1 jit_solution(12925280043253956362)
XLA Ops:
  0.6 2.2 %own_tile.1 = (f32[4624,128]{1,0:T(8,128)S(1)}, f32[592,128]{1,0:T(8,128)S(1)}, f32[576,128]{1,0:T(8,128)S(1)}, f32[576,128]{1,0:T(8,128)S(1)}, f32[576,128]{1,0:T(8,128)S(1)}, /*index=5*/f32[576,128]{1,0:T(8,128)S(1)}) custom-call(f32[8,16,16,128]{3,2,1,0:T(8,128)} %basis_hbm.1, s32[16,16,128]{2,1,0:T(8,128)} %labels_hbm.1, s32[16,16,128]{2,1,0:T(8,128)} %support_hbm.1, ...), custom_call_target="tpu_custom_call" | custom-call | tf_op jit(solution)/shard_map/own_tile/pallas_call | solution.py:485
  2.9 2.2 %collective-permute-start = (f32[576,128]{1,0:T(8,128)S(1)}, f32[576,128]{1,0:T(8,128)S(1)}, u32[]{:S(2)}, u32[]{:S(2)}) collective-permute-start(f32[576,128]{1,0:T(8,128)S(1)} %get-tuple-element.21), channel_id=1, source_target_pairs={{0,8},{8,0},{16,24},{24,16},{1,9},{9,1},{17,25},{25,17},{2,10},{10... | collective-permute-start | bytes 884744 | tf_op jit(solution)/shard_map/ppermute | solution.py:462
  5.1 0.7 %collective-permute-start.1 = (f32[576,128]{1,0:T(8,128)S(1)}, f32[576,128]{1,0:T(8,128)S(1)}, u32[]{:S(2)}, u32[]{:S(2)}) collective-permute-start(f32[576,128]{1,0:T(8,128)S(1)} %get-tuple-element.22), channel_id=1, source_target_pairs={{8,16},{16,8},{9,17},{17,9},{10,18},{18,10},{11,19},{19,11},{12,20... | collective-permute-start | bytes 884744 | tf_op jit(solution)/shard_map/ppermute | solution.py:463
  5.8 1.0 %collective-permute-start.4 = (f32[576,128]{1,0:T(8,128)S(1)}, f32[576,128]{1,0:T(8,128)S(1)}, u32[]{:S(2)}, u32[]{:S(2)}) collective-permute-start(f32[576,128]{1,0:T(8,128)S(1)} %get-tuple-element.28), channel_id=1, source_target_pairs={{0,1},{1,0},{2,3},{3,2},{4,5},{5,4},{6,7},{7,6},{8,9},{9,8},{10,11... | collective-permute-start | bytes 884744 | tf_op jit(solution)/shard_map/ppermute | solution.py:462
  6.8 3.0 %collective-permute-start.5 = (f32[576,128]{1,0:T(8,128)S(1)}, f32[576,128]{1,0:T(8,128)S(1)}, u32[]{:S(2)}, u32[]{:S(2)}) collective-permute-start(f32[576,128]{1,0:T(8,128)S(1)} %get-tuple-element.29), channel_id=1, source_target_pairs={{1,2},{2,1},{3,4},{4,3},{5,6},{6,5},{9,10},{10,9},{11,12},{12,11},... | collective-permute-start | bytes 884744 | tf_op jit(solution)/shard_map/ppermute | solution.py:463
  9.8 2.6 %inner_stage.1 = (f32[4624,128]{1,0:T(8,128)S(1)}, f32[4624,128]{1,0:T(8,128)S(1)}, f32[7,592,128]{2,1,0:T(8,128)S(1)}, f32[64,128]{1,0:T(8,128)S(1)}) custom-call(f32[4624,128]{1,0:T(8,128)S(1)} %get-tuple-element.23.field_in, f32[592,128]{1,0:T(8,128)S(1)} %get-tuple-element.24.perm.refs_4_), custom_call_target="tpu_custom_call", output_to_operand_aliasing={{0}: (0, {})} | custom-call | flops 10485760 | bytes 8388608 | tf_op jit(solution)/shard_map/inner_stage/pallas_call | solution.py:502
  12.4 0.0 collective-permute-done.from_a.refs_0_
  12.4 0.0 collective-permute-done.1.from_b.refs_1_
  12.4 0.7 %collective-permute-start.2 = (f32[112,128]{1,0:T(8,128)S(1)}, f32[112,128]{1,0:T(8,128)S(1)}, u32[]{:S(2)}, u32[]{:S(2)}) collective-permute-start(f32[112,128]{1,0:T(8,128)S(1)} %get-tuple-element.26), channel_id=1, source_target_pairs={{0,1},{1,0},{2,3},{3,2},{4,5},{5,4},{6,7},{7,6},{8,9},{9,8},{10,11... | collective-permute-start | bytes 172040 | tf_op jit(solution)/shard_map/ppermute | solution.py:462
  13.1 3.2 %collective-permute-start.3 = (f32[112,128]{1,0:T(8,128)S(1)}, f32[112,128]{1,0:T(8,128)S(1)}, u32[]{:S(2)}, u32[]{:S(2)}) collective-permute-start(f32[112,128]{1,0:T(8,128)S(1)} %get-tuple-element.27), channel_id=1, source_target_pairs={{1,2},{2,1},{3,4},{4,3},{5,6},{6,5},{9,10},{10,9},{11,12},{12,11},... | collective-permute-start | bytes 172040 | tf_op jit(solution)/shard_map/ppermute | solution.py:463
  16.3 0.0 collective-permute-done.4.refs_2_
  16.3 1.3 %collective-permute-done.5.refs_3_ = f32[576,128]{1,0:T(8,128)S(1)} collective-permute-done((f32[576,128]{1,0:T(8,128)S(1)}, f32[576,128]{1,0:T(8,128)S(1)}, u32[]{:S(2)}, u32[]{:S(2)}) %collective-permute-start.5) | collective-permute-done | bytes 294944 | tf_op jit(solution)/shard_map/ppermute | solution.py:463
  17.7 3.9 %strip_stage.1 = (f32[592,128]{1,0:T(8,128)S(1)}, f32[4624,128]{1,0:T(8,128)S(1)}, f32[4624,128]{1,0:T(8,128)S(1)}, f32[7,592,128]{2,1,0:T(8,128)S(1)}, f32[64,128]{1,0:T(8,128)S(1)}) custom-call(f32[576,128]{1,0:T(8,128)S(1)} %collective-permute-done.from_a.refs_0_, ...), custom_call_target="tpu_custom_call", output_to_operand_aliasing={{0}: (4, {}), {1}: (5, {}), {2}: (6, {}), {3}: (7, {}), {4}... | custom-call | flops 10485760 | bytes 8388608 | tf_op jit(solution)/shard_map/strip_stage/pallas_call | solution.py:522
  21.5 0.0 collective-permute-done.2.refs_0_
  21.6 0.0 collective-permute-done.3.refs_1_
  21.6 1.6 %corner_stage.1 = (f32[8,128]{1,0:T(8,128)S(1)}, f32[592,128]{1,0:T(8,128)S(1)}, f32[4624,128]{1,0:T(8,128)S(1)}, f32[4624,128]{1,0:T(8,128)S(1)}, f32[7,592,128]{2,1,0:T(8,128)S(1)}) custom-call(f32[112,128]{1,0:T(8,128)S(1)} %collective-permute-done.2.refs_0_, ...), custom_call_target="tpu_custom_call", output_to_operand_aliasing={{1}: (2, {}), {2}: (3, {}), {3}: (4, {}), {4}: (5, {})} | custom-call | tf_op jit(solution)/shard_map/corner_stage/pallas_call | solution.py:532
  23.1 5.5 %collective-permute-start.8 = (f32[8,128]{1,0:T(8,128)S(1)}, f32[8,128]{1,0:T(8,128)S(1)}, u32[]{:S(2)}, u32[]{:S(2)}) collective-permute-start(f32[8,128]{1,0:T(8,128)S(1)} %get-tuple-element.39), channel_id=1, source_target_pairs={{0,9},{1,10},{2,11},{3,12},{4,13},{5,14},{6,15},{8,17},{9,18},{10,... | collective-permute-start | bytes 12296 | tf_op jit(solution)/shard_map/ppermute | solution.py:474
  28.7 4.4 %collective-permute-start.7 = (f32[8,128]{1,0:T(8,128)S(1)}, f32[8,128]{1,0:T(8,128)S(1)}, u32[]{:S(2)}, u32[]{:S(2)}) collective-permute-start(f32[8,128]{1,0:T(8,128)S(1)} %get-tuple-element.39), channel_id=1, source_target_pairs={{0,1},{1,2},{2,3},{3,4},{4,5},{5,6},{6,7},{8,9},{9,10},{10,11},{11... | collective-permute-start | bytes 12296 | tf_op jit(solution)/shard_map/ppermute | solution.py:474
  33.1 1.7 %collective-permute-start.6 = (f32[8,128]{1,0:T(8,128)S(1)}, f32[8,128]{1,0:T(8,128)S(1)}, u32[]{:S(2)}, u32[]{:S(2)}) collective-permute-start(f32[8,128]{1,0:T(8,128)S(1)} %get-tuple-element.39), channel_id=1, source_target_pairs={{0,8},{1,9},{2,10},{3,11},{4,12},{5,13},{6,14},{7,15},{8,16},{9,17... | collective-permute-start | bytes 12296 | tf_op jit(solution)/shard_map/ppermute | solution.py:474
  34.8 1.6 %basis_out.1 = f32[8,16,16,128]{3,2,1,0:T(8,128)} custom-call(f32[4624,128]{1,0:T(8,128)S(1)} %get-tuple-element.38.field), custom_call_target="tpu_custom_call" | custom-call | bytes 2097152 | tf_op jit(solution)/shard_map/basis_out/pallas_call | solution.py:544
  36.5 0.0 collective-permute-done.8
  36.5 0.0 collective-permute-done.7
  36.5 0.0 collective-permute-done.6
  36.5 0.7 %add_bitcast_fusion = f32[27,1,1,8]{0,3,2,1:T(8,128)} fusion(f32[8,128]{1,0:T(8,128)S(1)} %collective-permute-done.8, f32[8,128]{1,0:T(8,128)S(1)} %collective-permute-done.7, f32[8,128]{1,0:T(8,128)S(1)} %collective-permute-done.6, f32[8,128]{1,0:T(8,128)S(1)} %get-tuple-element.39), kind=kLoop, calls=%fused_computation | loop fusion | flops 648 | bytes 4320 | tf_op jit(solution)/shard_map/reshape | solution.py:554
  (1 shorter events, 0.0 us)
Async XLA Ops:
  2.9 9.5 %collective-permute-start = (f32[576,128]{1,0:T(8,128)S(1)}, f32[576,128]{1,0:T(8,128)S(1)}, u32[]{:S(2)}, u32[]{:S(2)}) collective-permute-start(f32[576,128]{1,0:T(8,128)S(1)} %get-tuple-element.21), channel_id=1, source_target_pairs={{0,8},{8,0},{16,24},{24,16},{1,9},{9,1},{17,25},{25,17},{2,10},{10... | collective-permute-start | bytes 884744 | tf_op jit(solution)/shard_map/ppermute | solution.py:462
  5.1 7.3 %collective-permute-start.1 = (f32[576,128]{1,0:T(8,128)S(1)}, f32[576,128]{1,0:T(8,128)S(1)}, u32[]{:S(2)}, u32[]{:S(2)}) collective-permute-start(f32[576,128]{1,0:T(8,128)S(1)} %get-tuple-element.22), channel_id=1, source_target_pairs={{8,16},{16,8},{9,17},{17,9},{10,18},{18,10},{11,19},{19,11},{12,20... | collective-permute-start | bytes 884744 | tf_op jit(solution)/shard_map/ppermute | solution.py:463
  5.8 10.6 %collective-permute-start.4 = (f32[576,128]{1,0:T(8,128)S(1)}, f32[576,128]{1,0:T(8,128)S(1)}, u32[]{:S(2)}, u32[]{:S(2)}) collective-permute-start(f32[576,128]{1,0:T(8,128)S(1)} %get-tuple-element.28), channel_id=1, source_target_pairs={{0,1},{1,0},{2,3},{3,2},{4,5},{5,4},{6,7},{7,6},{8,9},{9,8},{10,11... | collective-permute-start | bytes 884744 | tf_op jit(solution)/shard_map/ppermute | solution.py:462
  6.8 10.9 %collective-permute-start.5 = (f32[576,128]{1,0:T(8,128)S(1)}, f32[576,128]{1,0:T(8,128)S(1)}, u32[]{:S(2)}, u32[]{:S(2)}) collective-permute-start(f32[576,128]{1,0:T(8,128)S(1)} %get-tuple-element.29), channel_id=1, source_target_pairs={{1,2},{2,1},{3,4},{4,3},{5,6},{6,5},{9,10},{10,9},{11,12},{12,11},... | collective-permute-start | bytes 884744 | tf_op jit(solution)/shard_map/ppermute | solution.py:463
  12.4 9.1 %collective-permute-start.2 = (f32[112,128]{1,0:T(8,128)S(1)}, f32[112,128]{1,0:T(8,128)S(1)}, u32[]{:S(2)}, u32[]{:S(2)}) collective-permute-start(f32[112,128]{1,0:T(8,128)S(1)} %get-tuple-element.26), channel_id=1, source_target_pairs={{0,1},{1,0},{2,3},{3,2},{4,5},{5,4},{6,7},{7,6},{8,9},{9,8},{10,11... | collective-permute-start | bytes 172040 | tf_op jit(solution)/shard_map/ppermute | solution.py:462
  13.1 8.4 %collective-permute-start.3 = (f32[112,128]{1,0:T(8,128)S(1)}, f32[112,128]{1,0:T(8,128)S(1)}, u32[]{:S(2)}, u32[]{:S(2)}) collective-permute-start(f32[112,128]{1,0:T(8,128)S(1)} %get-tuple-element.27), channel_id=1, source_target_pairs={{1,2},{2,1},{3,4},{4,3},{5,6},{6,5},{9,10},{10,9},{11,12},{12,11},... | collective-permute-start | bytes 172040 | tf_op jit(solution)/shard_map/ppermute | solution.py:463
  23.1 13.3 %collective-permute-start.8 = (f32[8,128]{1,0:T(8,128)S(1)}, f32[8,128]{1,0:T(8,128)S(1)}, u32[]{:S(2)}, u32[]{:S(2)}) collective-permute-start(f32[8,128]{1,0:T(8,128)S(1)} %get-tuple-element.39), channel_id=1, source_target_pairs={{0,9},{1,10},{2,11},{3,12},{4,13},{5,14},{6,15},{8,17},{9,18},{10,... | collective-permute-start | bytes 12296 | tf_op jit(solution)/shard_map/ppermute | solution.py:474
  28.7 7.8 %collective-permute-start.7 = (f32[8,128]{1,0:T(8,128)S(1)}, f32[8,128]{1,0:T(8,128)S(1)}, u32[]{:S(2)}, u32[]{:S(2)}) collective-permute-start(f32[8,128]{1,0:T(8,128)S(1)} %get-tuple-element.39), channel_id=1, source_target_pairs={{0,1},{1,2},{2,3},{3,4},{4,5},{5,6},{6,7},{8,9},{9,10},{10,11},{11... | collective-permute-start | bytes 12296 | tf_op jit(solution)/shard_map/ppermute | solution.py:474
  33.1 3.3 %collective-permute-start.6 = (f32[8,128]{1,0:T(8,128)S(1)}, f32[8,128]{1,0:T(8,128)S(1)}, u32[]{:S(2)}, u32[]{:S(2)}) collective-permute-start(f32[8,128]{1,0:T(8,128)S(1)} %get-tuple-element.39), channel_id=1, source_target_pairs={{0,8},{1,9},{2,10},{3,11},{4,12},{5,13},{6,14},{7,15},{8,16},{9,17... | collective-permute-start | bytes 12296 | tf_op jit(solution)/shard_map/ppermute | solution.py:474

commit v2 on v1

--- a/solution.py
+++ b/solution.py
@@ -17,6 +17,7 @@
 FACE = DEPTH * CB
 CORNER = tuple((i, j) for i in range(1, DEPTH) for j in range(1, DEPTH) if i + j <= DEPTH)
 MIB = 1 << 20
+FIRST_PAIRS = {"gx": 1, "gy": 0}
 F32 = jnp.float32
 
 step_share = 2.0 / 3.0
@@ -67,7 +68,7 @@
 
 
 def is_even(axis):
-    return lax.rem(lax.axis_index(axis), 2) == 0
+    return lax.rem(lax.axis_index(axis), 2) == FIRST_PAIRS[axis]
 
 
 def look_up(label, table):
@@ -459,8 +460,8 @@
 
 def swap_both(first, second, axis):
     return (
-        lax.ppermute(first, axis, swap_pairs(axis, 0)),
-        lax.ppermute(second, axis, swap_pairs(axis, 1)),
+        lax.ppermute(first, axis, swap_pairs(axis, FIRST_PAIRS[axis])),
+        lax.ppermute(second, axis, swap_pairs(axis, 1 - FIRST_PAIRS[axis])),
     )
 
 

time: 37.4 us -> 36.3 us (0.971)
  starting transfers between devices: 22.5 us -> 21.6 us
    ppermute x3, starting transfers between devices: 11.7 us -> 7.83 us  [ahead(): return lax.ppermute(array, ('gx', 'gy'), pairs)]
    ppermute x6, starting transfers between devices: 10.8 us -> 13.8 us  [the longest x3 10.7 us: swap_both(): lax.ppermute(second, axis, swap_pairs(axis, 1 - FIRST_PAIRS[axis]))]
where the time goes in v2:
time: 36.3 us; the launch traced here: 36 us
  starting transfers between devices  21.6 us (60%)
  Pallas kernels  11.9 us (33%)
  waiting for transfers between devices  1.08 us (3%)
  between operations  0.76 us (2%)
  other arithmetic  0.67 us (2%)
    ppermute x3, starting transfers between devices, swap_both(): lax.ppermute(second, axis, swap_pairs(axis, 1 - FIRST_PAIRS[axis]))  10.7 us
    ppermute x3, starting transfers between devices, ahead(): return lax.ppermute(array, ('gx', 'gy'), pairs)  7.83 us
    pallas_call x1, Pallas kernels, shards(): pl.pallas_call(strip_kernel, out_shape=(in_vmem(*PLAIN), in_vmem(*FIELD),...  3.86 us
    ppermute x3, starting transfers between devices, swap_both(): lax.ppermute(first, axis, swap_pairs(axis, FIRST_PAIRS[axis]))  3.09 us
    pallas_call x1, Pallas kernels, shards(): pl.pallas_call(inner_kernel, out_shape=(in_vmem(*FIELD), in_vmem(*FIELD),...  2.56 us
    pallas_call x1, Pallas kernels, shards(): pl.pallas_call(own_kernel, out_shape=(in_vmem(*FIELD), in_vmem(*PLAIN), f...  2.25 us
    pallas_call x1, Pallas kernels, shards(): pl.pallas_call(basis_kernel, out_shape=jax.ShapeDtypeStruct((SLOTS, CB, C...  1.62 us
    pallas_call x1, Pallas kernels, shards(): pl.pallas_call(last_kernel, out_shape=(in_vmem(8, LANES), in_vmem(*PLAIN)...  1.56 us
  transfers between devices with their start and end apart: 9, of which 1 were waited for; matrix products, arithmetic and copies ran while one was open for 0% of the time, Pallas kernels for 22%

profile of v2, /device:TPU:1, one launch (start us, length us, event | category | flops | bytes accessed | tf_op | source)
XLA Modules:
  0.0 36.0 jit_solution(10496317275753238528)
XLA Ops:
  0.6 2.2 %own_tile.1 = (f32[4624,128]{1,0:T(8,128)S(1)}, f32[592,128]{1,0:T(8,128)S(1)}, f32[576,128]{1,0:T(8,128)S(1)}, f32[576,128]{1,0:T(8,128)S(1)}, f32[576,128]{1,0:T(8,128)S(1)}, /*index=5*/f32[576,128]{1,0:T(8,128)S(1)}) custom-call(f32[8,16,16,128]{3,2,1,0:T(8,128)} %basis_hbm.1, s32[16,16,128]{2,1,0:T(8,128)} %labels_hbm.1, s32[16,16,128]{2,1,0:T(8,128)} %support_hbm.1, ...), custom_call_target="tpu_custom_call" | custom-call | tf_op jit(solution)/shard_map/own_tile/pallas_call | solution.py:486
  2.9 0.7 %collective-permute-start = (f32[576,128]{1,0:T(8,128)S(1)}, f32[576,128]{1,0:T(8,128)S(1)}, u32[]{:S(2)}, u32[]{:S(2)}) collective-permute-start(f32[576,128]{1,0:T(8,128)S(1)} %get-tuple-element.21), channel_id=1, source_target_pairs={{8,16},{16,8},{9,17},{17,9},{10,18},{18,10},{11,19},{19,11},{12,20... | collective-permute-start | bytes 884744 | tf_op jit(solution)/shard_map/ppermute | solution.py:463
  3.6 4.7 %collective-permute-start.1 = (f32[576,128]{1,0:T(8,128)S(1)}, f32[576,128]{1,0:T(8,128)S(1)}, u32[]{:S(2)}, u32[]{:S(2)}) collective-permute-start(f32[576,128]{1,0:T(8,128)S(1)} %get-tuple-element.22), channel_id=1, source_target_pairs={{0,8},{8,0},{16,24},{24,16},{1,9},{9,1},{17,25},{25,17},{2,10},{10... | collective-permute-start | bytes 884744 | tf_op jit(solution)/shard_map/ppermute | solution.py:464
  8.3 1.2 %collective-permute-start.4 = (f32[576,128]{1,0:T(8,128)S(1)}, f32[576,128]{1,0:T(8,128)S(1)}, u32[]{:S(2)}, u32[]{:S(2)}) collective-permute-start(f32[576,128]{1,0:T(8,128)S(1)} %get-tuple-element.28), channel_id=1, source_target_pairs={{0,1},{1,0},{2,3},{3,2},{4,5},{5,4},{6,7},{7,6},{8,9},{9,8},{10,11... | collective-permute-start | bytes 884744 | tf_op jit(solution)/shard_map/ppermute | solution.py:463
  9.5 3.0 %collective-permute-start.5 = (f32[576,128]{1,0:T(8,128)S(1)}, f32[576,128]{1,0:T(8,128)S(1)}, u32[]{:S(2)}, u32[]{:S(2)}) collective-permute-start(f32[576,128]{1,0:T(8,128)S(1)} %get-tuple-element.29), channel_id=1, source_target_pairs={{1,2},{2,1},{3,4},{4,3},{5,6},{6,5},{9,10},{10,9},{11,12},{12,11},... | collective-permute-start | bytes 884744 | tf_op jit(solution)/shard_map/ppermute | solution.py:464
  12.5 2.6 %inner_stage.1 = (f32[4624,128]{1,0:T(8,128)S(1)}, f32[4624,128]{1,0:T(8,128)S(1)}, f32[7,592,128]{2,1,0:T(8,128)S(1)}, f32[64,128]{1,0:T(8,128)S(1)}) custom-call(f32[4624,128]{1,0:T(8,128)S(1)} %get-tuple-element.23.field_in, f32[592,128]{1,0:T(8,128)S(1)} %get-tuple-element.24.perm.refs_4_), custom_call_target="tpu_custom_call", output_to_operand_aliasing={{0}: (0, {})} | custom-call | flops 10485760 | bytes 8388608 | tf_op jit(solution)/shard_map/inner_stage/pallas_call | solution.py:503
  15.1 0.0 collective-permute-done.from_a.refs_0_
  15.1 0.0 collective-permute-done.1.from_b.refs_1_
  15.2 1.2 %collective-permute-start.2 = (f32[112,128]{1,0:T(8,128)S(1)}, f32[112,128]{1,0:T(8,128)S(1)}, u32[]{:S(2)}, u32[]{:S(2)}) collective-permute-start(f32[112,128]{1,0:T(8,128)S(1)} %get-tuple-element.26), channel_id=1, source_target_pairs={{0,1},{1,0},{2,3},{3,2},{4,5},{5,4},{6,7},{7,6},{8,9},{9,8},{10,11... | collective-permute-start | bytes 172040 | tf_op jit(solution)/shard_map/ppermute | solution.py:463
  16.3 3.0 %collective-permute-start.3 = (f32[112,128]{1,0:T(8,128)S(1)}, f32[112,128]{1,0:T(8,128)S(1)}, u32[]{:S(2)}, u32[]{:S(2)}) collective-permute-start(f32[112,128]{1,0:T(8,128)S(1)} %get-tuple-element.27), channel_id=1, source_target_pairs={{1,2},{2,1},{3,4},{4,3},{5,6},{6,5},{9,10},{10,9},{11,12},{12,11},... | collective-permute-start | bytes 172040 | tf_op jit(solution)/shard_map/ppermute | solution.py:464
  19.4 0.0 collective-permute-done.4.refs_2_
  19.4 1.1 %collective-permute-done.5.refs_3_ = f32[576,128]{1,0:T(8,128)S(1)} collective-permute-done((f32[576,128]{1,0:T(8,128)S(1)}, f32[576,128]{1,0:T(8,128)S(1)}, u32[]{:S(2)}, u32[]{:S(2)}) %collective-permute-start.5) | collective-permute-done | bytes 294944 | tf_op jit(solution)/shard_map/ppermute | solution.py:464
  20.4 3.9 %strip_stage.1 = (f32[592,128]{1,0:T(8,128)S(1)}, f32[4624,128]{1,0:T(8,128)S(1)}, f32[4624,128]{1,0:T(8,128)S(1)}, f32[7,592,128]{2,1,0:T(8,128)S(1)}, f32[64,128]{1,0:T(8,128)S(1)}) custom-call(f32[576,128]{1,0:T(8,128)S(1)} %collective-permute-done.from_a.refs_0_, ...), custom_call_target="tpu_custom_call", output_to_operand_aliasing={{0}: (4, {}), {1}: (5, {}), {2}: (6, {}), {3}: (7, {}), {4}... | custom-call | flops 10485760 | bytes 8388608 | tf_op jit(solution)/shard_map/strip_stage/pallas_call | solution.py:523
  24.3 0.0 collective-permute-done.2.refs_0_
  24.3 0.0 collective-permute-done.3.refs_1_
  24.3 1.6 %corner_stage.1 = (f32[8,128]{1,0:T(8,128)S(1)}, f32[592,128]{1,0:T(8,128)S(1)}, f32[4624,128]{1,0:T(8,128)S(1)}, f32[4624,128]{1,0:T(8,128)S(1)}, f32[7,592,128]{2,1,0:T(8,128)S(1)}) custom-call(f32[112,128]{1,0:T(8,128)S(1)} %collective-permute-done.2.refs_0_, ...), custom_call_target="tpu_custom_call", output_to_operand_aliasing={{1}: (2, {}), {2}: (3, {}), {3}: (4, {}), {4}: (5, {})} | custom-call | tf_op jit(solution)/shard_map/corner_stage/pallas_call | solution.py:533
  25.9 2.7 %collective-permute-start.8 = (f32[8,128]{1,0:T(8,128)S(1)}, f32[8,128]{1,0:T(8,128)S(1)}, u32[]{:S(2)}, u32[]{:S(2)}) collective-permute-start(f32[8,128]{1,0:T(8,128)S(1)} %get-tuple-element.39), channel_id=1, source_target_pairs={{0,9},{1,10},{2,11},{3,12},{4,13},{5,14},{6,15},{8,17},{9,18},{10,... | collective-permute-start | bytes 12296 | tf_op jit(solution)/shard_map/ppermute | solution.py:475
  28.6 3.1 %collective-permute-start.7 = (f32[8,128]{1,0:T(8,128)S(1)}, f32[8,128]{1,0:T(8,128)S(1)}, u32[]{:S(2)}, u32[]{:S(2)}) collective-permute-start(f32[8,128]{1,0:T(8,128)S(1)} %get-tuple-element.39), channel_id=1, source_target_pairs={{0,1},{1,2},{2,3},{3,4},{4,5},{5,6},{6,7},{8,9},{9,10},{10,11},{11... | collective-permute-start | bytes 12296 | tf_op jit(solution)/shard_map/ppermute | solution.py:475
  31.7 2.1 %collective-permute-start.6 = (f32[8,128]{1,0:T(8,128)S(1)}, f32[8,128]{1,0:T(8,128)S(1)}, u32[]{:S(2)}, u32[]{:S(2)}) collective-permute-start(f32[8,128]{1,0:T(8,128)S(1)} %get-tuple-element.39), channel_id=1, source_target_pairs={{0,8},{1,9},{2,10},{3,11},{4,12},{5,13},{6,14},{7,15},{8,16},{9,17... | collective-permute-start | bytes 12296 | tf_op jit(solution)/shard_map/ppermute | solution.py:475
  33.7 1.6 %basis_out.1 = f32[8,16,16,128]{3,2,1,0:T(8,128)} custom-call(f32[4624,128]{1,0:T(8,128)S(1)} %get-tuple-element.38.field), custom_call_target="tpu_custom_call" | custom-call | bytes 2097152 | tf_op jit(solution)/shard_map/basis_out/pallas_call | solution.py:545
  35.4 0.0 collective-permute-done.8
  35.4 0.0 collective-permute-done.7
  35.4 0.0 collective-permute-done.6
  35.4 0.7 %add_bitcast_fusion = f32[27,1,1,8]{0,3,2,1:T(8,128)} fusion(f32[8,128]{1,0:T(8,128)S(1)} %collective-permute-done.8, f32[8,128]{1,0:T(8,128)S(1)} %collective-permute-done.7, f32[8,128]{1,0:T(8,128)S(1)} %collective-permute-done.6, f32[8,128]{1,0:T(8,128)S(1)} %get-tuple-element.39), kind=kLoop, calls=%fused_computation | loop fusion | flops 648 | bytes 4320 | tf_op jit(solution)/shard_map/reshape | solution.py:555
  (1 shorter events, 0.0 us)
Async XLA Ops:
  2.9 12.2 %collective-permute-start = (f32[576,128]{1,0:T(8,128)S(1)}, f32[576,128]{1,0:T(8,128)S(1)}, u32[]{:S(2)}, u32[]{:S(2)}) collective-permute-start(f32[576,128]{1,0:T(8,128)S(1)} %get-tuple-element.21), channel_id=1, source_target_pairs={{8,16},{16,8},{9,17},{17,9},{10,18},{18,10},{11,19},{19,11},{12,20... | collective-permute-start | bytes 884744 | tf_op jit(solution)/shard_map/ppermute | solution.py:463
  3.6 11.5 %collective-permute-start.1 = (f32[576,128]{1,0:T(8,128)S(1)}, f32[576,128]{1,0:T(8,128)S(1)}, u32[]{:S(2)}, u32[]{:S(2)}) collective-permute-start(f32[576,128]{1,0:T(8,128)S(1)} %get-tuple-element.22), channel_id=1, source_target_pairs={{0,8},{8,0},{16,24},{24,16},{1,9},{9,1},{17,25},{25,17},{2,10},{10... | collective-permute-start | bytes 884744 | tf_op jit(solution)/shard_map/ppermute | solution.py:464
  8.3 11.1 %collective-permute-start.4 = (f32[576,128]{1,0:T(8,128)S(1)}, f32[576,128]{1,0:T(8,128)S(1)}, u32[]{:S(2)}, u32[]{:S(2)}) collective-permute-start(f32[576,128]{1,0:T(8,128)S(1)} %get-tuple-element.28), channel_id=1, source_target_pairs={{0,1},{1,0},{2,3},{3,2},{4,5},{5,4},{6,7},{7,6},{8,9},{9,8},{10,11... | collective-permute-start | bytes 884744 | tf_op jit(solution)/shard_map/ppermute | solution.py:463
  9.5 10.9 %collective-permute-start.5 = (f32[576,128]{1,0:T(8,128)S(1)}, f32[576,128]{1,0:T(8,128)S(1)}, u32[]{:S(2)}, u32[]{:S(2)}) collective-permute-start(f32[576,128]{1,0:T(8,128)S(1)} %get-tuple-element.29), channel_id=1, source_target_pairs={{1,2},{2,1},{3,4},{4,3},{5,6},{6,5},{9,10},{10,9},{11,12},{12,11},... | collective-permute-start | bytes 884744 | tf_op jit(solution)/shard_map/ppermute | solution.py:464
  15.2 9.1 %collective-permute-start.2 = (f32[112,128]{1,0:T(8,128)S(1)}, f32[112,128]{1,0:T(8,128)S(1)}, u32[]{:S(2)}, u32[]{:S(2)}) collective-permute-start(f32[112,128]{1,0:T(8,128)S(1)} %get-tuple-element.26), channel_id=1, source_target_pairs={{0,1},{1,0},{2,3},{3,2},{4,5},{5,4},{6,7},{7,6},{8,9},{9,8},{10,11... | collective-permute-start | bytes 172040 | tf_op jit(solution)/shard_map/ppermute | solution.py:463
  16.3 8.0 %collective-permute-start.3 = (f32[112,128]{1,0:T(8,128)S(1)}, f32[112,128]{1,0:T(8,128)S(1)}, u32[]{:S(2)}, u32[]{:S(2)}) collective-permute-start(f32[112,128]{1,0:T(8,128)S(1)} %get-tuple-element.27), channel_id=1, source_target_pairs={{1,2},{2,1},{3,4},{4,3},{5,6},{6,5},{9,10},{10,9},{11,12},{12,11},... | collective-permute-start | bytes 172040 | tf_op jit(solution)/shard_map/ppermute | solution.py:464
  25.9 9.5 %collective-permute-start.8 = (f32[8,128]{1,0:T(8,128)S(1)}, f32[8,128]{1,0:T(8,128)S(1)}, u32[]{:S(2)}, u32[]{:S(2)}) collective-permute-start(f32[8,128]{1,0:T(8,128)S(1)} %get-tuple-element.39), channel_id=1, source_target_pairs={{0,9},{1,10},{2,11},{3,12},{4,13},{5,14},{6,15},{8,17},{9,18},{10,... | collective-permute-start | bytes 12296 | tf_op jit(solution)/shard_map/ppermute | solution.py:475
  28.6 6.8 %collective-permute-start.7 = (f32[8,128]{1,0:T(8,128)S(1)}, f32[8,128]{1,0:T(8,128)S(1)}, u32[]{:S(2)}, u32[]{:S(2)}) collective-permute-start(f32[8,128]{1,0:T(8,128)S(1)} %get-tuple-element.39), channel_id=1, source_target_pairs={{0,1},{1,2},{2,3},{3,4},{4,5},{5,6},{6,7},{8,9},{9,10},{10,11},{11... | collective-permute-start | bytes 12296 | tf_op jit(solution)/shard_map/ppermute | solution.py:475
  31.7 3.7 %collective-permute-start.6 = (f32[8,128]{1,0:T(8,128)S(1)}, f32[8,128]{1,0:T(8,128)S(1)}, u32[]{:S(2)}, u32[]{:S(2)}) collective-permute-start(f32[8,128]{1,0:T(8,128)S(1)} %get-tuple-element.39), channel_id=1, source_target_pairs={{0,8},{1,9},{2,10},{3,11},{4,12},{5,13},{6,14},{7,15},{8,16},{9,17... | collective-permute-start | bytes 12296 | tf_op jit(solution)/shard_map/ppermute | solution.py:475

commit v3 on v2

--- a/solution.py
+++ b/solution.py
@@ -115,8 +115,6 @@
 
     lax.fori_loop(0, CB, one_perm, 0, unroll=4)
     fetch_support.wait()
-    for copy in fetch_basis:
-        copy.wait()
     basis = basis.reshape(SLOTS * CB * CB, LANES)
     support = support.reshape(CB * CB, LANES)
 
@@ -128,7 +126,9 @@
             )
         return 0
 
-    lax.fori_loop(0, CB, one_x, 0, unroll=2)
+    for part, copy in enumerate(fetch_basis):
+        copy.wait()
+        lax.fori_loop(DEPTH * part, DEPTH * (part + 1), one_x, 0, unroll=2)
 
     def x_face(out, start):
         out[SLOTS * FACE : FACE_ROWS, :] = jnp.concatenate(
@@ -313,11 +313,11 @@
     lax.fori_loop(0, 2, some_coef, 0)
 
     def cells_at(level, i):
-        return [(i + u, y) for u in range(CB // 2 - level) for y in range(level, CB - level)]
+        return [(i + u, y) for u in range(CB - 2 * level) for y in range(level, CB - level)]
 
     zero = jnp.zeros((8, LANES), F32)
     sums = run_stage(
-        coef, field_a, field_b, (zero,) * SLOTS, cells_at, lambda level: (level, 2, CB // 2 - level)
+        coef, field_a, field_b, (zero,) * SLOTS, cells_at, lambda level: (level, 1, CB - 2 * level)
     )
     for s in range(SLOTS):
         acc[8 * s : 8 * s + 8, :] = sums[s]
@@ -366,10 +366,10 @@
 
     def cells_at(level, i):
         across = list(range(level - DEPTH, level)) + list(range(CB - level, CB - level + DEPTH))
-        return [c for u in range(CB // 2 - level) for c in [(x, i + u) for x in across] + [(i + u, y) for y in across]]
+        return [c for u in range(CB - 2 * level) for c in [(x, i + u) for x in across] + [(i + u, y) for y in across]]
 
     sums = tuple(acc[8 * s : 8 * s + 8, :] for s in range(SLOTS))
-    sums = run_stage(coef, field_a, field_b, sums, cells_at, lambda level: (level, 2, CB // 2 - level))
+    sums = run_stage(coef, field_a, field_b, sums, cells_at, lambda level: (level, 1, CB - 2 * level))
     for s in range(SLOTS):
         acc[8 * s : 8 * s + 8, :] = sums[s]
 
@@ -439,15 +439,24 @@
     )
 
 
-def basis_kernel(field, out):
+def basis_kernel(field, out_hbm, out, sems):
     flat = out.reshape(SLOTS * CB * CB, LANES)
+    copies = [
+        pltpu.make_async_copy(out.at[part], out_hbm.at[:, pl.ds(DEPTH * part, DEPTH)], sems.at[part])
+        for part in range(CB // DEPTH)
+    ]
 
     def one_x(x, _):
         for y in range(CB):
-            flat[pl.ds(x * CB + y, SLOTS, stride=CB * CB), :] = field[pl.ds(aligned(field_row(x, y)), SLOTS), :]
+            start = (x // DEPTH) * (SLOTS * FACE) + (x % DEPTH) * CB + y
+            flat[pl.ds(start, SLOTS, stride=FACE), :] = field[pl.ds(aligned(field_row(x, y)), SLOTS), :]
         return 0
 
-    lax.fori_loop(0, CB, one_x, 0)
+    for part, copy in enumerate(copies):
+        lax.fori_loop(DEPTH * part, DEPTH * (part + 1), one_x, 0, unroll=2)
+        copy.start()
+    for copy in copies:
+        copy.wait()
 
 
 def swap_pairs(axis, first):
@@ -546,7 +555,11 @@
         basis_kernel,
         out_shape=jax.ShapeDtypeStruct((SLOTS, CB, CB, LANES), F32),
         in_specs=[VMEM_SPEC],
-        out_specs=VMEM_SPEC,
+        out_specs=HBM_SPEC,
+        scratch_shapes=[
+            pltpu.VMEM((CB // DEPTH, SLOTS, DEPTH, CB, LANES), F32),
+            pltpu.SemaphoreType.DMA((CB // DEPTH,)),
+        ],
         compiler_params=params(4),
         cost_estimate=pl.CostEstimate(flops=0, bytes_accessed=2 * MIB, transcendentals=0),
         name="basis_out",

time: 36.3 us -> 35.4 us (0.975)
  Pallas kernels: 11.9 us -> 10.4 us
  starting transfers between devices: 21.6 us -> 22.1 us
    pallas_call x1, Pallas kernels: 3.86 us -> 3.34 us  [shards(): pl.pallas_call(strip_kernel, out_shape=(in_vmem(*PLAIN), in_vmem(*FIELD),...]
    pallas_call x1, Pallas kernels: 2.56 us -> 2.1 us  [shards(): pl.pallas_call(inner_kernel, out_shape=(in_vmem(*FIELD), in_vmem(*FIELD),...]
    ppermute x3, starting transfers between devices: 3.09 us -> 3.53 us  [swap_both(): lax.ppermute(first, axis, swap_pairs(axis, FIRST_PAIRS[axis]))]
  transfers between devices with their start and end apart: 9 -> 9, of which waited for: 1 -> 2; matrix products, arithmetic and copies ran while one was open for 0% -> 0% of each run, Pallas kernels for 22% -> 20%
where the time goes in v3:
time: 35.4 us; the launch traced here: 35.1 us
  starting transfers between devices  22.1 us (62%)
  Pallas kernels  10.4 us (29%)
  waiting for transfers between devices  1.13 us (3%)
  between operations  0.77 us (2%)
  other arithmetic  0.67 us (2%)
    ppermute x3, starting transfers between devices, swap_both(): lax.ppermute(second, axis, swap_pairs(axis, 1 - FIRST_PAIRS[axis]))  10.7 us
    ppermute x3, starting transfers between devices, ahead(): return lax.ppermute(array, ('gx', 'gy'), pairs)  7.83 us
    ppermute x3, starting transfers between devices, swap_both(): lax.ppermute(first, axis, swap_pairs(axis, FIRST_PAIRS[axis]))  3.53 us
    pallas_call x1, Pallas kernels, shards(): pl.pallas_call(strip_kernel, out_shape=(in_vmem(*PLAIN), in_vmem(*FIELD),...  3.34 us
    pallas_call x1, Pallas kernels, shards(): pl.pallas_call(inner_kernel, out_shape=(in_vmem(*FIELD), in_vmem(*FIELD),...  2.1 us
    pallas_call x1, Pallas kernels, shards(): pl.pallas_call(own_kernel, out_shape=(in_vmem(*FIELD), in_vmem(*PLAIN), f...  2.01 us
    pallas_call x1, Pallas kernels, shards(): pl.pallas_call(last_kernel, out_shape=(in_vmem(8, LANES), in_vmem(*PLAIN)...  1.56 us
    pallas_call x1, Pallas kernels, shards(): pl.pallas_call(basis_kernel, out_shape=jax.ShapeDtypeStruct((SLOTS, CB, C...  1.4 us
  transfers between devices with their start and end apart: 9, of which 2 were waited for; matrix products, arithmetic and copies ran while one was open for 0% of the time, Pallas kernels for 20%

profile of v3, /device:TPU:1, one launch (start us, length us, event | category | flops | bytes accessed | tf_op | source)
XLA Modules:
  0.0 35.1 jit_solution(8079743293137861660)
XLA Ops:
  0.6 2.0 %own_tile.1 = (f32[4624,128]{1,0:T(8,128)S(1)}, f32[592,128]{1,0:T(8,128)S(1)}, f32[576,128]{1,0:T(8,128)S(1)}, f32[576,128]{1,0:T(8,128)S(1)}, f32[576,128]{1,0:T(8,128)S(1)}, /*index=5*/f32[576,128]{1,0:T(8,128)S(1)}) custom-call(f32[8,16,16,128]{3,2,1,0:T(8,128)} %basis_hbm.1, s32[16,16,128]{2,1,0:T(8,128)} %labels_hbm.1, s32[16,16,128]{2,1,0:T(8,128)} %support_hbm.1, ...), custom_call_target="tpu_custom_call" | custom-call | tf_op jit(solution)/shard_map/own_tile/pallas_call | solution.py:495
  2.6 0.7 %collective-permute-start = (f32[576,128]{1,0:T(8,128)S(1)}, f32[576,128]{1,0:T(8,128)S(1)}, u32[]{:S(2)}, u32[]{:S(2)}) collective-permute-start(f32[576,128]{1,0:T(8,128)S(1)} %get-tuple-element.21), channel_id=1, source_target_pairs={{8,16},{16,8},{9,17},{17,9},{10,18},{18,10},{11,19},{19,11},{12,20... | collective-permute-start | bytes 884744 | tf_op jit(solution)/shard_map/ppermute | solution.py:472
  3.3 4.7 %collective-permute-start.1 = (f32[576,128]{1,0:T(8,128)S(1)}, f32[576,128]{1,0:T(8,128)S(1)}, u32[]{:S(2)}, u32[]{:S(2)}) collective-permute-start(f32[576,128]{1,0:T(8,128)S(1)} %get-tuple-element.22), channel_id=1, source_target_pairs={{0,8},{8,0},{16,24},{24,16},{1,9},{9,1},{17,25},{25,17},{2,10},{10... | collective-permute-start | bytes 884744 | tf_op jit(solution)/shard_map/ppermute | solution.py:473
  8.1 1.2 %collective-permute-start.4 = (f32[576,128]{1,0:T(8,128)S(1)}, f32[576,128]{1,0:T(8,128)S(1)}, u32[]{:S(2)}, u32[]{:S(2)}) collective-permute-start(f32[576,128]{1,0:T(8,128)S(1)} %get-tuple-element.28), channel_id=1, source_target_pairs={{0,1},{1,0},{2,3},{3,2},{4,5},{5,4},{6,7},{7,6},{8,9},{9,8},{10,11... | collective-permute-start | bytes 884744 | tf_op jit(solution)/shard_map/ppermute | solution.py:472
  9.3 3.0 %collective-permute-start.5 = (f32[576,128]{1,0:T(8,128)S(1)}, f32[576,128]{1,0:T(8,128)S(1)}, u32[]{:S(2)}, u32[]{:S(2)}) collective-permute-start(f32[576,128]{1,0:T(8,128)S(1)} %get-tuple-element.29), channel_id=1, source_target_pairs={{1,2},{2,1},{3,4},{4,3},{5,6},{6,5},{9,10},{10,9},{11,12},{12,11},... | collective-permute-start | bytes 884744 | tf_op jit(solution)/shard_map/ppermute | solution.py:473
  12.3 2.1 %inner_stage.1 = (f32[4624,128]{1,0:T(8,128)S(1)}, f32[4624,128]{1,0:T(8,128)S(1)}, f32[7,592,128]{2,1,0:T(8,128)S(1)}, f32[64,128]{1,0:T(8,128)S(1)}) custom-call(f32[4624,128]{1,0:T(8,128)S(1)} %get-tuple-element.23.field_in, f32[592,128]{1,0:T(8,128)S(1)} %get-tuple-element.24.perm.refs_4_), custom_call_target="tpu_custom_call", output_to_operand_aliasing={{0}: (0, {})} | custom-call | flops 10485760 | bytes 8388608 | tf_op jit(solution)/shard_map/inner_stage/pallas_call | solution.py:512
  14.4 0.0 collective-permute-done.from_a.refs_0_
  14.4 0.1 collective-permute-done.1.from_b.refs_1_
  14.5 1.6 %collective-permute-start.2 = (f32[112,128]{1,0:T(8,128)S(1)}, f32[112,128]{1,0:T(8,128)S(1)}, u32[]{:S(2)}, u32[]{:S(2)}) collective-permute-start(f32[112,128]{1,0:T(8,128)S(1)} %get-tuple-element.26), channel_id=1, source_target_pairs={{0,1},{1,0},{2,3},{3,2},{4,5},{5,4},{6,7},{7,6},{8,9},{9,8},{10,11... | collective-permute-start | bytes 172040 | tf_op jit(solution)/shard_map/ppermute | solution.py:472
  16.1 3.0 %collective-permute-start.3 = (f32[112,128]{1,0:T(8,128)S(1)}, f32[112,128]{1,0:T(8,128)S(1)}, u32[]{:S(2)}, u32[]{:S(2)}) collective-permute-start(f32[112,128]{1,0:T(8,128)S(1)} %get-tuple-element.27), channel_id=1, source_target_pairs={{1,2},{2,1},{3,4},{4,3},{5,6},{6,5},{9,10},{10,9},{11,12},{12,11},... | collective-permute-start | bytes 172040 | tf_op jit(solution)/shard_map/ppermute | solution.py:473
  19.1 0.0 collective-permute-done.4.refs_2_
  19.1 1.1 %collective-permute-done.5.refs_3_ = f32[576,128]{1,0:T(8,128)S(1)} collective-permute-done((f32[576,128]{1,0:T(8,128)S(1)}, f32[576,128]{1,0:T(8,128)S(1)}, u32[]{:S(2)}, u32[]{:S(2)}) %collective-permute-start.5) | collective-permute-done | bytes 294944 | tf_op jit(solution)/shard_map/ppermute | solution.py:473
  20.2 3.3 %strip_stage.1 = (f32[592,128]{1,0:T(8,128)S(1)}, f32[4624,128]{1,0:T(8,128)S(1)}, f32[4624,128]{1,0:T(8,128)S(1)}, f32[7,592,128]{2,1,0:T(8,128)S(1)}, f32[64,128]{1,0:T(8,128)S(1)}) custom-call(f32[576,128]{1,0:T(8,128)S(1)} %collective-permute-done.from_a.refs_0_, ...), custom_call_target="tpu_custom_call", output_to_operand_aliasing={{0}: (4, {}), {1}: (5, {}), {2}: (6, {}), {3}: (7, {}), {4}... | custom-call | flops 10485760 | bytes 8388608 | tf_op jit(solution)/shard_map/strip_stage/pallas_call | solution.py:532
  23.6 0.0 collective-permute-done.2.refs_0_
  23.6 0.0 collective-permute-done.3.refs_1_
  23.6 1.6 %corner_stage.1 = (f32[8,128]{1,0:T(8,128)S(1)}, f32[592,128]{1,0:T(8,128)S(1)}, f32[4624,128]{1,0:T(8,128)S(1)}, f32[4624,128]{1,0:T(8,128)S(1)}, f32[7,592,128]{2,1,0:T(8,128)S(1)}) custom-call(f32[112,128]{1,0:T(8,128)S(1)} %collective-permute-done.2.refs_0_, ...), custom_call_target="tpu_custom_call", output_to_operand_aliasing={{1}: (2, {}), {2}: (3, {}), {3}: (4, {}), {4}: (5, {})} | custom-call | tf_op jit(solution)/shard_map/corner_stage/pallas_call | solution.py:542
  25.1 2.7 %collective-permute-start.8 = (f32[8,128]{1,0:T(8,128)S(1)}, f32[8,128]{1,0:T(8,128)S(1)}, u32[]{:S(2)}, u32[]{:S(2)}) collective-permute-start(f32[8,128]{1,0:T(8,128)S(1)} %get-tuple-element.39), channel_id=1, source_target_pairs={{0,9},{1,10},{2,11},{3,12},{4,13},{5,14},{6,15},{8,17},{9,18},{10,... | collective-permute-start | bytes 12296 | tf_op jit(solution)/shard_map/ppermute | solution.py:484
  27.8 3.1 %collective-permute-start.7 = (f32[8,128]{1,0:T(8,128)S(1)}, f32[8,128]{1,0:T(8,128)S(1)}, u32[]{:S(2)}, u32[]{:S(2)}) collective-permute-start(f32[8,128]{1,0:T(8,128)S(1)} %get-tuple-element.39), channel_id=1, source_target_pairs={{0,1},{1,2},{2,3},{3,4},{4,5},{5,6},{6,7},{8,9},{9,10},{10,11},{11... | collective-permute-start | bytes 12296 | tf_op jit(solution)/shard_map/ppermute | solution.py:484
  30.9 2.1 %collective-permute-start.6 = (f32[8,128]{1,0:T(8,128)S(1)}, f32[8,128]{1,0:T(8,128)S(1)}, u32[]{:S(2)}, u32[]{:S(2)}) collective-permute-start(f32[8,128]{1,0:T(8,128)S(1)} %get-tuple-element.39), channel_id=1, source_target_pairs={{0,8},{1,9},{2,10},{3,11},{4,12},{5,13},{6,14},{7,15},{8,16},{9,17... | collective-permute-start | bytes 12296 | tf_op jit(solution)/shard_map/ppermute | solution.py:484
  33.0 1.4 %basis_out.1 = f32[8,16,16,128]{3,2,1,0:T(8,128)} custom-call(f32[4624,128]{1,0:T(8,128)S(1)} %get-tuple-element.38.field), custom_call_target="tpu_custom_call" | custom-call | bytes 2097152 | tf_op jit(solution)/shard_map/basis_out/pallas_call | solution.py:554
  34.4 0.0 collective-permute-done.8
  34.4 0.0 collective-permute-done.7
  34.4 0.0 collective-permute-done.6
  34.4 0.7 %add_bitcast_fusion = f32[27,1,1,8]{0,3,2,1:T(8,128)} fusion(f32[8,128]{1,0:T(8,128)S(1)} %collective-permute-done.8, f32[8,128]{1,0:T(8,128)S(1)} %collective-permute-done.7, f32[8,128]{1,0:T(8,128)S(1)} %collective-permute-done.6, f32[8,128]{1,0:T(8,128)S(1)} %get-tuple-element.39), kind=kLoop, calls=%fused_computation | loop fusion | flops 648 | bytes 4320 | tf_op jit(solution)/shard_map/reshape | solution.py:568
  (1 shorter events, 0.0 us)
Async XLA Ops:
  2.6 11.8 %collective-permute-start = (f32[576,128]{1,0:T(8,128)S(1)}, f32[576,128]{1,0:T(8,128)S(1)}, u32[]{:S(2)}, u32[]{:S(2)}) collective-permute-start(f32[576,128]{1,0:T(8,128)S(1)} %get-tuple-element.21), channel_id=1, source_target_pairs={{8,16},{16,8},{9,17},{17,9},{10,18},{18,10},{11,19},{19,11},{12,20... | collective-permute-start | bytes 884744 | tf_op jit(solution)/shard_map/ppermute | solution.py:472
  3.3 11.1 %collective-permute-start.1 = (f32[576,128]{1,0:T(8,128)S(1)}, f32[576,128]{1,0:T(8,128)S(1)}, u32[]{:S(2)}, u32[]{:S(2)}) collective-permute-start(f32[576,128]{1,0:T(8,128)S(1)} %get-tuple-element.22), channel_id=1, source_target_pairs={{0,8},{8,0},{16,24},{24,16},{1,9},{9,1},{17,25},{25,17},{2,10},{10... | collective-permute-start | bytes 884744 | tf_op jit(solution)/shard_map/ppermute | solution.py:473
  8.1 11.1 %collective-permute-start.4 = (f32[576,128]{1,0:T(8,128)S(1)}, f32[576,128]{1,0:T(8,128)S(1)}, u32[]{:S(2)}, u32[]{:S(2)}) collective-permute-start(f32[576,128]{1,0:T(8,128)S(1)} %get-tuple-element.28), channel_id=1, source_target_pairs={{0,1},{1,0},{2,3},{3,2},{4,5},{5,4},{6,7},{7,6},{8,9},{9,8},{10,11... | collective-permute-start | bytes 884744 | tf_op jit(solution)/shard_map/ppermute | solution.py:472
  9.3 10.9 %collective-permute-start.5 = (f32[576,128]{1,0:T(8,128)S(1)}, f32[576,128]{1,0:T(8,128)S(1)}, u32[]{:S(2)}, u32[]{:S(2)}) collective-permute-start(f32[576,128]{1,0:T(8,128)S(1)} %get-tuple-element.29), channel_id=1, source_target_pairs={{1,2},{2,1},{3,4},{4,3},{5,6},{6,5},{9,10},{10,9},{11,12},{12,11},... | collective-permute-start | bytes 884744 | tf_op jit(solution)/shard_map/ppermute | solution.py:473
  14.5 9.1 %collective-permute-start.2 = (f32[112,128]{1,0:T(8,128)S(1)}, f32[112,128]{1,0:T(8,128)S(1)}, u32[]{:S(2)}, u32[]{:S(2)}) collective-permute-start(f32[112,128]{1,0:T(8,128)S(1)} %get-tuple-element.26), channel_id=1, source_target_pairs={{0,1},{1,0},{2,3},{3,2},{4,5},{5,4},{6,7},{7,6},{8,9},{9,8},{10,11... | collective-permute-start | bytes 172040 | tf_op jit(solution)/shard_map/ppermute | solution.py:472
  16.1 7.5 %collective-permute-start.3 = (f32[112,128]{1,0:T(8,128)S(1)}, f32[112,128]{1,0:T(8,128)S(1)}, u32[]{:S(2)}, u32[]{:S(2)}) collective-permute-start(f32[112,128]{1,0:T(8,128)S(1)} %get-tuple-element.27), channel_id=1, source_target_pairs={{1,2},{2,1},{3,4},{4,3},{5,6},{6,5},{9,10},{10,9},{11,12},{12,11},... | collective-permute-start | bytes 172040 | tf_op jit(solution)/shard_map/ppermute | solution.py:473
  25.1 9.3 %collective-permute-start.8 = (f32[8,128]{1,0:T(8,128)S(1)}, f32[8,128]{1,0:T(8,128)S(1)}, u32[]{:S(2)}, u32[]{:S(2)}) collective-permute-start(f32[8,128]{1,0:T(8,128)S(1)} %get-tuple-element.39), channel_id=1, source_target_pairs={{0,9},{1,10},{2,11},{3,12},{4,13},{5,14},{6,15},{8,17},{9,18},{10,... | collective-permute-start | bytes 12296 | tf_op jit(solution)/shard_map/ppermute | solution.py:484
  27.8 6.6 %collective-permute-start.7 = (f32[8,128]{1,0:T(8,128)S(1)}, f32[8,128]{1,0:T(8,128)S(1)}, u32[]{:S(2)}, u32[]{:S(2)}) collective-permute-start(f32[8,128]{1,0:T(8,128)S(1)} %get-tuple-element.39), channel_id=1, source_target_pairs={{0,1},{1,2},{2,3},{3,4},{4,5},{5,6},{6,7},{8,9},{9,10},{10,11},{11... | collective-permute-start | bytes 12296 | tf_op jit(solution)/shard_map/ppermute | solution.py:484
  30.9 3.5 %collective-permute-start.6 = (f32[8,128]{1,0:T(8,128)S(1)}, f32[8,128]{1,0:T(8,128)S(1)}, u32[]{:S(2)}, u32[]{:S(2)}) collective-permute-start(f32[8,128]{1,0:T(8,128)S(1)} %get-tuple-element.39), channel_id=1, source_target_pairs={{0,8},{1,9},{2,10},{3,11},{4,12},{5,13},{6,14},{7,15},{8,16},{9,17... | collective-permute-start | bytes 12296 | tf_op jit(solution)/shard_map/ppermute | solution.py:484

commit v4 on v3

--- a/solution.py
+++ b/solution.py
@@ -92,15 +92,25 @@
     return jnp.where(found != 0, basis[pl.ds(start, SLOTS, stride=stride), :], 0.0)
 
 
-def own_kernel(
-    basis_hbm, labels_hbm, support_hbm, table_hbm, field, perm, x_a, x_b, y_a, y_b, basis, labels, support, table, sems
+def fill_field(field, basis, part, support, bits, x):
+    for y in range(CB):
+        start = part * (SLOTS * FACE) + (x % DEPTH) * CB + y
+        field[pl.ds(aligned(field_row(x, y)), SLOTS), :] = first_weights(
+            basis, start, FACE, support[pl.ds(x * CB + y, 1), :], bits
+        )
+
+
+def x_face_kernel(
+    basis_hbm, labels_hbm, support_hbm, table_hbm, field, perm, x_a, x_b, middle, support, ends, labels, table, sems
 ):
     fetch_table = pltpu.make_async_copy(table_hbm, table, sems.at[0])
     fetch_labels = pltpu.make_async_copy(labels_hbm, labels, sems.at[1])
     fetch_support = pltpu.make_async_copy(support_hbm, support, sems.at[2])
     fetch_basis = [
-        pltpu.make_async_copy(basis_hbm.at[:, pl.ds(DEPTH * part, DEPTH)], basis.at[part], sems.at[3 + part])
-        for part in range(CB // DEPTH)
+        pltpu.make_async_copy(basis_hbm.at[:, pl.ds(start, DEPTH)], into, sems.at[3 + n])
+        for n, (start, into) in enumerate(
+            ((0, ends.at[0]), (CB - DEPTH, ends.at[1]), (DEPTH, middle.at[0]), (2 * DEPTH, middle.at[1]))
+        )
     ]
     for copy in (fetch_table, fetch_labels, fetch_support, *fetch_basis):
         copy.start()
@@ -115,20 +125,16 @@
 
     lax.fori_loop(0, CB, one_perm, 0, unroll=4)
     fetch_support.wait()
-    basis = basis.reshape(SLOTS * CB * CB, LANES)
+    flat = ends.reshape(2 * SLOTS * FACE, LANES)
     support = support.reshape(CB * CB, LANES)
-
-    def one_x(x, _):
-        for y in range(CB):
-            start = (x // DEPTH) * (SLOTS * FACE) + (x % DEPTH) * CB + y
-            field[pl.ds(aligned(field_row(x, y)), SLOTS), :] = first_weights(
-                basis, start, FACE, support[pl.ds(x * CB + y, 1), :], bits
-            )
-        return 0
-
-    for part, copy in enumerate(fetch_basis):
-        copy.wait()
-        lax.fori_loop(DEPTH * part, DEPTH * (part + 1), one_x, 0, unroll=2)
+    for part, start in enumerate((0, CB - DEPTH)):
+        fetch_basis[part].wait()
+
+        def one_x(x, _, part=part):
+            fill_field(field, flat, part, support, bits, x)
+            return 0
+
+        lax.fori_loop(start, start + DEPTH, one_x, 0, unroll=2)
 
     def x_face(out, start):
         out[SLOTS * FACE : FACE_ROWS, :] = jnp.concatenate(
@@ -138,6 +144,31 @@
             rows = CB * SLOTS
             out[x * rows : (x + 1) * rows, :] = field[field_row(start + x, 0) : field_row(start + x, CB), :]
 
+    for even in (True, False):
+
+        @pl.when(is_even("gx") == even)
+        def _(even=even):
+            high, low = (x_a, x_b) if even else (x_b, x_a)
+            x_face(low, 0)
+            x_face(high, CB - DEPTH)
+
+    for copy in fetch_basis[2:]:
+        copy.wait()
+
+
+def y_face_kernel(field_in, perm, middle, support, field, y_a, y_b):
+    del field_in
+    bits = slot_bits()
+    flat = middle.reshape(2 * SLOTS * FACE, LANES)
+    support = support.reshape(CB * CB, LANES)
+    for part in range(2):
+
+        def one_x(x, _, part=part):
+            fill_field(field, flat, part, support, bits, x)
+            return 0
+
+        lax.fori_loop(DEPTH * (part + 1), DEPTH * (part + 2), one_x, 0, unroll=2)
+
     def y_face(out, start):
         rows = DEPTH * SLOTS
         for x in range(CB):
@@ -146,12 +177,6 @@
             out[x * rows : (x + 1) * rows, :] = field[field_row(x, start) : field_row(x, start + DEPTH), :]
 
     for even in (True, False):
-
-        @pl.when(is_even("gx") == even)
-        def _(even=even):
-            high, low = (x_a, x_b) if even else (x_b, x_a)
-            x_face(low, 0)
-            x_face(high, CB - DEPTH)
 
         @pl.when(is_even("gy") == even)
         def _(even=even):
@@ -186,10 +211,10 @@
     return 2.0 * one * two / jnp.maximum(one + two, 1e-30)
 
 
-def fill_coef(perm, coef, xs):
+def fill_coef(perm, coef, xs, tiles=(0, 1, 2)):
     lane = lane_iota()
     for x in xs:
-        for tile in range(3):
+        for tile in tiles:
             at = aligned(column(x, 8 * tile - DEPTH))
             here = perm[pl.ds(at, 8), :]
             x_up = conductance(here, perm[pl.ds(at + PAD, 8), :])
@@ -359,8 +384,10 @@
             lax.fori_loop(0, CB, one_x, 0)
 
     def some_coef(n, _):
-        fill_coef(perm, coef, [11 * n + 1 - DEPTH + u for u in range(11)])
+        fill_coef(perm, coef, [1 + 7 * n + u for u in range(7)], (0, 2))
         return 0
+
+    fill_coef(perm, coef, [*range(1 - DEPTH, 1), *range(CB - 1, CB + DEPTH - 1)])
 
     lax.fori_loop(0, 2, some_coef, 0)
 
@@ -492,22 +519,32 @@
     size_x, size_y, size_z = labels.shape
     assert (size_x, size_y, size_z) == (CB, CB, LANES)
     face = in_vmem(FACE_ROWS, LANES)
-    field, perm, x_face_a, x_face_b, y_face_a, y_face_b = pl.pallas_call(
-        own_kernel,
-        out_shape=(in_vmem(*FIELD), in_vmem(*PLAIN), face, face, face, face),
+    half = (2, SLOTS, DEPTH, CB, LANES)
+    bits = pltpu.VMEM((CB, CB, LANES), jnp.int32)
+    field, perm, x_face_a, x_face_b, middle, held = pl.pallas_call(
+        x_face_kernel,
+        out_shape=(in_vmem(*FIELD), in_vmem(*PLAIN), face, face, in_vmem(*half), bits),
         in_specs=[HBM_SPEC] * 4,
         out_specs=(VMEM_SPEC,) * 6,
         scratch_shapes=[
-            pltpu.VMEM((CB // DEPTH, SLOTS, DEPTH, CB, LANES), F32),
-            pltpu.VMEM((CB, CB, LANES), jnp.int32),
+            pltpu.VMEM(half, F32),
             pltpu.VMEM((CB, CB, LANES), jnp.int32),
             pltpu.SMEM((NCLASS,), F32),
-            pltpu.SemaphoreType.DMA((3 + CB // DEPTH,)),
+            pltpu.SemaphoreType.DMA((7,)),
         ],
         compiler_params=params(4),
-        name="own_tile",
+        name="x_faces",
     )(*[in_hbm(a) for a in (initial_basis, labels, support, class_perm)])
     x_a, x_b = swap_both(x_face_a, x_face_b, "gx")
+    field, y_face_a, y_face_b = pl.pallas_call(
+        y_face_kernel,
+        out_shape=(in_vmem(*FIELD), face, face),
+        in_specs=[VMEM_SPEC] * 4,
+        out_specs=(VMEM_SPEC,) * 3,
+        input_output_aliases={0: 0},
+        compiler_params=params(4),
+        name="y_faces",
+    )(pinned(field), pinned(perm), pinned(middle), pinned(held))
     y_a, y_b = swap_both(y_face_a, y_face_b, "gy")
     field_a, field_b, coef, acc = pl.pallas_call(
         inner_kernel,

time: 35.4 us -> 35.2 us (level)
  starting transfers between devices: 22.1 us -> 21.6 us
  waiting for transfers between devices: 1.13 us -> 1.55 us
    ppermute x3, starting transfers between devices: 3.53 us -> 3.1 us  [swap_both(): lax.ppermute(first, axis, swap_pairs(axis, FIRST_PAIRS[axis]))]
    ppermute x3, waiting for transfers between devices: 1.12 us -> 1.54 us  [swap_both(): lax.ppermute(second, axis, swap_pairs(axis, 1 - FIRST_PAIRS[axis]))]
    pallas_call x1 -> x2, Pallas kernels: 2.01 us -> 1.98 us  [the longest x1 1.56 us: shards(): pl.pallas_call(x_face_kernel, out_shape=(in_vmem(*FIELD), in_vmem(*PLAIN)...]
  transfers between devices with their start and end apart: 9 -> 9, of which waited for: 2 -> 1; matrix products, arithmetic and copies ran while one was open for 0% -> 0% of each run, Pallas kernels for 20% -> 21%
where the time goes in v4:
time: 35.2 us; the launch traced here: 35 us
  starting transfers between devices  21.6 us (61%)
  Pallas kernels  10.4 us (30%)
  waiting for transfers between devices  1.55 us (4%)
  between operations  0.79 us (2%)
  other arithmetic  0.67 us (2%)
    ppermute x3, starting transfers between devices, swap_both(): lax.ppermute(second, axis, swap_pairs(axis, 1 - FIRST_PAIRS[axis]))  10.8 us
    ppermute x3, starting transfers between devices, ahead(): return lax.ppermute(array, ('gx', 'gy'), pairs)  7.71 us
    pallas_call x1, Pallas kernels, shards(): pl.pallas_call(strip_kernel, out_shape=(in_vmem(*PLAIN), in_vmem(*FIELD),...  3.31 us
    ppermute x3, starting transfers between devices, swap_both(): lax.ppermute(first, axis, swap_pairs(axis, FIRST_PAIRS[axis]))  3.1 us
    pallas_call x1, Pallas kernels, shards(): pl.pallas_call(inner_kernel, out_shape=(in_vmem(*FIELD), in_vmem(*FIELD),...  2.1 us
    pallas_call x1, Pallas kernels, shards(): pl.pallas_call(x_face_kernel, out_shape=(in_vmem(*FIELD), in_vmem(*PLAIN)...  1.56 us
    pallas_call x1, Pallas kernels, shards(): pl.pallas_call(last_kernel, out_shape=(in_vmem(8, LANES), in_vmem(*PLAIN)...  1.56 us
    ppermute x3, waiting for transfers between devices, swap_both(): lax.ppermute(second, axis, swap_pairs(axis, 1 - FIRST_PAIRS[axis]))  1.54 us
  transfers between devices with their start and end apart: 9, of which 1 were waited for; matrix products, arithmetic and copies ran while one was open for 0% of the time, Pallas kernels for 21%

profile of v4, /device:TPU:1, one launch (start us, length us, event | category | flops | bytes accessed | tf_op | source)
XLA Modules:
  0.0 35.0 jit_solution(4527173332415741045)
XLA Ops:
  0.6 1.6 %x_faces.1 = (f32[4624,128]{1,0:T(8,128)S(1)}, f32[592,128]{1,0:T(8,128)S(1)}, f32[576,128]{1,0:T(8,128)S(1)}, f32[576,128]{1,0:T(8,128)S(1)}, f32[2,8,4,16,128]...) custom-call(f32[8,16,16,128]{3,2,1,0:T(8,128)} %basis_hbm.1, s32[16,16,128]{2,1,0:T(8,128)} %labels_hbm.1, ...), custom_call_target="tpu_custom_call" | custom-call | tf_op jit(solution)/shard_map/x_faces/pallas_call | solution.py:524
  2.2 0.7 %collective-permute-start = (f32[576,128]{1,0:T(8,128)S(1)}, f32[576,128]{1,0:T(8,128)S(1)}, u32[]{:S(2)}, u32[]{:S(2)}) collective-permute-start(f32[576,128]{1,0:T(8,128)S(1)} %get-tuple-element.24), channel_id=1, source_target_pairs={{8,16},{16,8},{9,17},{17,9},{10,18},{18,10},{11,19},{19,11},{12,20... | collective-permute-start | bytes 884744 | tf_op jit(solution)/shard_map/ppermute | solution.py:499
  2.9 4.7 %collective-permute-start.1 = (f32[576,128]{1,0:T(8,128)S(1)}, f32[576,128]{1,0:T(8,128)S(1)}, u32[]{:S(2)}, u32[]{:S(2)}) collective-permute-start(f32[576,128]{1,0:T(8,128)S(1)} %get-tuple-element.25), channel_id=1, source_target_pairs={{0,8},{8,0},{16,24},{24,16},{1,9},{9,1},{17,25},{25,17},{2,10},{10... | collective-permute-start | bytes 884744 | tf_op jit(solution)/shard_map/ppermute | solution.py:500
  7.6 0.4 %y_faces.1 = (f32[4624,128]{1,0:T(8,128)S(1)}, f32[576,128]{1,0:T(8,128)S(1)}, f32[576,128]{1,0:T(8,128)S(1)}) custom-call(f32[4624,128]{1,0:T(8,128)S(1)} %get-tuple-element.26.field_in, f32[592,128]{1,0:T(8,128)S(1)} %get-tuple-element.27.perm.refs_4_, f32[2,8,4,16,128]{4,3,2,1,0:T(8,128)S(1)} %get-tuple-element.28.middle, ...), custom_call_target="tpu_custom_call", output_to_operand_aliasing={{0}: (0, {})} | custom-call | tf_op jit(solution)/shard_map/y_faces/pallas_call | solution.py:539
  8.0 1.3 %collective-permute-start.4 = (f32[576,128]{1,0:T(8,128)S(1)}, f32[576,128]{1,0:T(8,128)S(1)}, u32[]{:S(2)}, u32[]{:S(2)}) collective-permute-start(f32[576,128]{1,0:T(8,128)S(1)} %get-tuple-element.34), channel_id=1, source_target_pairs={{0,1},{1,0},{2,3},{3,2},{4,5},{5,4},{6,7},{7,6},{8,9},{9,8},{10,11... | collective-permute-start | bytes 884744 | tf_op jit(solution)/shard_map/ppermute | solution.py:499
  9.3 3.0 %collective-permute-start.5 = (f32[576,128]{1,0:T(8,128)S(1)}, f32[576,128]{1,0:T(8,128)S(1)}, u32[]{:S(2)}, u32[]{:S(2)}) collective-permute-start(f32[576,128]{1,0:T(8,128)S(1)} %get-tuple-element.35), channel_id=1, source_target_pairs={{1,2},{2,1},{3,4},{4,3},{5,6},{6,5},{9,10},{10,9},{11,12},{12,11},... | collective-permute-start | bytes 884744 | tf_op jit(solution)/shard_map/ppermute | solution.py:500
  12.4 2.1 %inner_stage.1 = (f32[4624,128]{1,0:T(8,128)S(1)}, f32[4624,128]{1,0:T(8,128)S(1)}, f32[7,592,128]{2,1,0:T(8,128)S(1)}, f32[64,128]{1,0:T(8,128)S(1)}) custom-call(f32[4624,128]{1,0:T(8,128)S(1)} %get-tuple-element.30.field_in, f32[592,128]{1,0:T(8,128)S(1)} %get-tuple-element.27.perm.refs_4_), custom_call_target="tpu_custom_call", output_to_operand_aliasing={{0}: (0, {})} | custom-call | flops 10485760 | bytes 8388608 | tf_op jit(solution)/shard_map/inner_stage/pallas_call | solution.py:549
  14.5 0.0 collective-permute-done.from_a.refs_0_
  14.5 0.0 collective-permute-done.1.from_b.refs_1_
  14.5 1.1 %collective-permute-start.2 = (f32[112,128]{1,0:T(8,128)S(1)}, f32[112,128]{1,0:T(8,128)S(1)}, u32[]{:S(2)}, u32[]{:S(2)}) collective-permute-start(f32[112,128]{1,0:T(8,128)S(1)} %get-tuple-element.32), channel_id=1, source_target_pairs={{0,1},{1,0},{2,3},{3,2},{4,5},{5,4},{6,7},{7,6},{8,9},{9,8},{10,11... | collective-permute-start | bytes 172040 | tf_op jit(solution)/shard_map/ppermute | solution.py:499
  15.7 3.0 %collective-permute-start.3 = (f32[112,128]{1,0:T(8,128)S(1)}, f32[112,128]{1,0:T(8,128)S(1)}, u32[]{:S(2)}, u32[]{:S(2)}) collective-permute-start(f32[112,128]{1,0:T(8,128)S(1)} %get-tuple-element.33), channel_id=1, source_target_pairs={{1,2},{2,1},{3,4},{4,3},{5,6},{6,5},{9,10},{10,9},{11,12},{12,11},... | collective-permute-start | bytes 172040 | tf_op jit(solution)/shard_map/ppermute | solution.py:500
  18.7 0.0 collective-permute-done.4.refs_2_
  18.7 1.5 %collective-permute-done.5.refs_3_ = f32[576,128]{1,0:T(8,128)S(1)} collective-permute-done((f32[576,128]{1,0:T(8,128)S(1)}, f32[576,128]{1,0:T(8,128)S(1)}, u32[]{:S(2)}, u32[]{:S(2)}) %collective-permute-start.5) | collective-permute-done | bytes 294944 | tf_op jit(solution)/shard_map/ppermute | solution.py:500
  20.2 3.3 %strip_stage.1 = (f32[592,128]{1,0:T(8,128)S(1)}, f32[4624,128]{1,0:T(8,128)S(1)}, f32[4624,128]{1,0:T(8,128)S(1)}, f32[7,592,128]{2,1,0:T(8,128)S(1)}, f32[64,128]{1,0:T(8,128)S(1)}) custom-call(f32[576,128]{1,0:T(8,128)S(1)} %collective-permute-done.from_a.refs_0_, ...), custom_call_target="tpu_custom_call", output_to_operand_aliasing={{0}: (4, {}), {1}: (5, {}), {2}: (6, {}), {3}: (7, {}), {4}... | custom-call | flops 10485760 | bytes 8388608 | tf_op jit(solution)/shard_map/strip_stage/pallas_call | solution.py:569
  23.5 0.0 collective-permute-done.2.refs_0_
  23.6 0.0 collective-permute-done.3.refs_1_
  23.6 1.6 %corner_stage.1 = (f32[8,128]{1,0:T(8,128)S(1)}, f32[592,128]{1,0:T(8,128)S(1)}, f32[4624,128]{1,0:T(8,128)S(1)}, f32[4624,128]{1,0:T(8,128)S(1)}, f32[7,592,128]{2,1,0:T(8,128)S(1)}) custom-call(f32[112,128]{1,0:T(8,128)S(1)} %collective-permute-done.2.refs_0_, ...), custom_call_target="tpu_custom_call", output_to_operand_aliasing={{1}: (2, {}), {2}: (3, {}), {3}: (4, {}), {4}: (5, {})} | custom-call | tf_op jit(solution)/shard_map/corner_stage/pallas_call | solution.py:579
  25.1 2.2 %collective-permute-start.8 = (f32[8,128]{1,0:T(8,128)S(1)}, f32[8,128]{1,0:T(8,128)S(1)}, u32[]{:S(2)}, u32[]{:S(2)}) collective-permute-start(f32[8,128]{1,0:T(8,128)S(1)} %get-tuple-element.45), channel_id=1, source_target_pairs={{0,9},{1,10},{2,11},{3,12},{4,13},{5,14},{6,15},{8,17},{9,18},{10,... | collective-permute-start | bytes 12296 | tf_op jit(solution)/shard_map/ppermute | solution.py:511
  27.4 3.4 %collective-permute-start.7 = (f32[8,128]{1,0:T(8,128)S(1)}, f32[8,128]{1,0:T(8,128)S(1)}, u32[]{:S(2)}, u32[]{:S(2)}) collective-permute-start(f32[8,128]{1,0:T(8,128)S(1)} %get-tuple-element.45), channel_id=1, source_target_pairs={{0,1},{1,2},{2,3},{3,4},{4,5},{5,6},{6,7},{8,9},{9,10},{10,11},{11... | collective-permute-start | bytes 12296 | tf_op jit(solution)/shard_map/ppermute | solution.py:511
  30.8 2.1 %collective-permute-start.6 = (f32[8,128]{1,0:T(8,128)S(1)}, f32[8,128]{1,0:T(8,128)S(1)}, u32[]{:S(2)}, u32[]{:S(2)}) collective-permute-start(f32[8,128]{1,0:T(8,128)S(1)} %get-tuple-element.45), channel_id=1, source_target_pairs={{0,8},{1,9},{2,10},{3,11},{4,12},{5,13},{6,14},{7,15},{8,16},{9,17... | collective-permute-start | bytes 12296 | tf_op jit(solution)/shard_map/ppermute | solution.py:511
  32.9 1.4 %basis_out.1 = f32[8,16,16,128]{3,2,1,0:T(8,128)} custom-call(f32[4624,128]{1,0:T(8,128)S(1)} %get-tuple-element.44.field), custom_call_target="tpu_custom_call" | custom-call | bytes 2097152 | tf_op jit(solution)/shard_map/basis_out/pallas_call | solution.py:591
  34.3 0.0 collective-permute-done.7
  34.3 0.0 collective-permute-done.6
  34.3 0.7 %add_bitcast_fusion = f32[27,1,1,8]{0,3,2,1:T(8,128)} fusion(f32[8,128]{1,0:T(8,128)S(1)} %collective-permute-done.8, f32[8,128]{1,0:T(8,128)S(1)} %collective-permute-done.7, f32[8,128]{1,0:T(8,128)S(1)} %collective-permute-done.6, f32[8,128]{1,0:T(8,128)S(1)} %get-tuple-element.45), kind=kLoop, calls=%fused_computation | loop fusion | flops 648 | bytes 4320 | tf_op jit(solution)/shard_map/reshape | solution.py:605
  (2 shorter events, 0.0 us)
Async XLA Ops:
  2.2 12.3 %collective-permute-start = (f32[576,128]{1,0:T(8,128)S(1)}, f32[576,128]{1,0:T(8,128)S(1)}, u32[]{:S(2)}, u32[]{:S(2)}) collective-permute-start(f32[576,128]{1,0:T(8,128)S(1)} %get-tuple-element.24), channel_id=1, source_target_pairs={{8,16},{16,8},{9,17},{17,9},{10,18},{18,10},{11,19},{19,11},{12,20... | collective-permute-start | bytes 884744 | tf_op jit(solution)/shard_map/ppermute | solution.py:499
  2.9 11.6 %collective-permute-start.1 = (f32[576,128]{1,0:T(8,128)S(1)}, f32[576,128]{1,0:T(8,128)S(1)}, u32[]{:S(2)}, u32[]{:S(2)}) collective-permute-start(f32[576,128]{1,0:T(8,128)S(1)} %get-tuple-element.25), channel_id=1, source_target_pairs={{0,8},{8,0},{16,24},{24,16},{1,9},{9,1},{17,25},{25,17},{2,10},{10... | collective-permute-start | bytes 884744 | tf_op jit(solution)/shard_map/ppermute | solution.py:500
  8.0 10.7 %collective-permute-start.4 = (f32[576,128]{1,0:T(8,128)S(1)}, f32[576,128]{1,0:T(8,128)S(1)}, u32[]{:S(2)}, u32[]{:S(2)}) collective-permute-start(f32[576,128]{1,0:T(8,128)S(1)} %get-tuple-element.34), channel_id=1, source_target_pairs={{0,1},{1,0},{2,3},{3,2},{4,5},{5,4},{6,7},{7,6},{8,9},{9,8},{10,11... | collective-permute-start | bytes 884744 | tf_op jit(solution)/shard_map/ppermute | solution.py:499
  9.3 10.9 %collective-permute-start.5 = (f32[576,128]{1,0:T(8,128)S(1)}, f32[576,128]{1,0:T(8,128)S(1)}, u32[]{:S(2)}, u32[]{:S(2)}) collective-permute-start(f32[576,128]{1,0:T(8,128)S(1)} %get-tuple-element.35), channel_id=1, source_target_pairs={{1,2},{2,1},{3,4},{4,3},{5,6},{6,5},{9,10},{10,9},{11,12},{12,11},... | collective-permute-start | bytes 884744 | tf_op jit(solution)/shard_map/ppermute | solution.py:500
  14.5 9.0 %collective-permute-start.2 = (f32[112,128]{1,0:T(8,128)S(1)}, f32[112,128]{1,0:T(8,128)S(1)}, u32[]{:S(2)}, u32[]{:S(2)}) collective-permute-start(f32[112,128]{1,0:T(8,128)S(1)} %get-tuple-element.32), channel_id=1, source_target_pairs={{0,1},{1,0},{2,3},{3,2},{4,5},{5,4},{6,7},{7,6},{8,9},{9,8},{10,11... | collective-permute-start | bytes 172040 | tf_op jit(solution)/shard_map/ppermute | solution.py:499
  15.7 7.9 %collective-permute-start.3 = (f32[112,128]{1,0:T(8,128)S(1)}, f32[112,128]{1,0:T(8,128)S(1)}, u32[]{:S(2)}, u32[]{:S(2)}) collective-permute-start(f32[112,128]{1,0:T(8,128)S(1)} %get-tuple-element.33), channel_id=1, source_target_pairs={{1,2},{2,1},{3,4},{4,3},{5,6},{6,5},{9,10},{10,9},{11,12},{12,11},... | collective-permute-start | bytes 172040 | tf_op jit(solution)/shard_map/ppermute | solution.py:500
  25.1 9.1 %collective-permute-start.8 = (f32[8,128]{1,0:T(8,128)S(1)}, f32[8,128]{1,0:T(8,128)S(1)}, u32[]{:S(2)}, u32[]{:S(2)}) collective-permute-start(f32[8,128]{1,0:T(8,128)S(1)} %get-tuple-element.45), channel_id=1, source_target_pairs={{0,9},{1,10},{2,11},{3,12},{4,13},{5,14},{6,15},{8,17},{9,18},{10,... | collective-permute-start | bytes 12296 | tf_op jit(solution)/shard_map/ppermute | solution.py:511
  27.4 6.9 %collective-permute-start.7 = (f32[8,128]{1,0:T(8,128)S(1)}, f32[8,128]{1,0:T(8,128)S(1)}, u32[]{:S(2)}, u32[]{:S(2)}) collective-permute-start(f32[8,128]{1,0:T(8,128)S(1)} %get-tuple-element.45), channel_id=1, source_target_pairs={{0,1},{1,2},{2,3},{3,4},{4,5},{5,6},{6,7},{8,9},{9,10},{10,11},{11... | collective-permute-start | bytes 12296 | tf_op jit(solution)/shard_map/ppermute | solution.py:511
  30.8 3.5 %collective-permute-start.6 = (f32[8,128]{1,0:T(8,128)S(1)}, f32[8,128]{1,0:T(8,128)S(1)}, u32[]{:S(2)}, u32[]{:S(2)}) collective-permute-start(f32[8,128]{1,0:T(8,128)S(1)} %get-tuple-element.45), channel_id=1, source_target_pairs={{0,8},{1,9},{2,10},{3,11},{4,12},{5,13},{6,14},{7,15},{8,16},{9,17... | collective-permute-start | bytes 12296 | tf_op jit(solution)/shard_map/ppermute | solution.py:511

commit v5 on v4

--- a/solution.py
+++ b/solution.py
@@ -348,9 +348,20 @@
         acc[8 * s : 8 * s + 8, :] = sums[s]
 
 
-def strip_kernel(*refs):
-    x_a, x_b, y_a, y_b = refs[:4]
-    perm, field_a, field_b, coef, acc = refs[9:]
+def strip_stage(coef, field_a, field_b, acc, cells_of):
+    def cells_at(level, i):
+        across = list(range(level - DEPTH, level)) + list(range(CB - level, CB - level + DEPTH))
+        return [c for u in range(CB - 2 * level) for c in cells_of(across, i + u)]
+
+    sums = tuple(acc[8 * s : 8 * s + 8, :] for s in range(SLOTS))
+    sums = run_stage(coef, field_a, field_b, sums, cells_at, lambda level: (level, 1, CB - 2 * level))
+    for s in range(SLOTS):
+        acc[8 * s : 8 * s + 8, :] = sums[s]
+
+
+def x_strip_kernel(*refs):
+    x_a, x_b = refs[:2]
+    perm, field_a, field_b, coef, acc = refs[7:]
 
     for even in (True, False):
 
@@ -369,6 +380,16 @@
 
                 lax.fori_loop(0, DEPTH, one_x, 0)
 
+    fill_coef(perm, coef, [*range(1 - DEPTH, 1), *range(CB - 1, CB + DEPTH - 1)])
+    strip_stage(coef, field_a, field_b, acc, lambda across, i: [(x, i) for x in across])
+
+
+def y_strip_kernel(*refs):
+    y_a, y_b = refs[:2]
+    perm, field_a, field_b, coef, acc = refs[7:]
+
+    for even in (True, False):
+
         @pl.when(is_even("gy") == even)
         def _(even=even):
             high, low = (y_a, y_b) if even else (y_b, y_a)
@@ -387,18 +408,8 @@
         fill_coef(perm, coef, [1 + 7 * n + u for u in range(7)], (0, 2))
         return 0
 
-    fill_coef(perm, coef, [*range(1 - DEPTH, 1), *range(CB - 1, CB + DEPTH - 1)])
-
     lax.fori_loop(0, 2, some_coef, 0)
-
-    def cells_at(level, i):
-        across = list(range(level - DEPTH, level)) + list(range(CB - level, CB - level + DEPTH))
-        return [c for u in range(CB - 2 * level) for c in [(x, i + u) for x in across] + [(i + u, y) for y in across]]
-
-    sums = tuple(acc[8 * s : 8 * s + 8, :] for s in range(SLOTS))
-    sums = run_stage(coef, field_a, field_b, sums, cells_at, lambda level: (level, 1, CB - 2 * level))
-    for s in range(SLOTS):
-        acc[8 * s : 8 * s + 8, :] = sums[s]
+    strip_stage(coef, field_a, field_b, acc, lambda across, i: [(i, y) for y in across])
 
 
 def node_tables():
@@ -566,16 +577,18 @@
         name="corners",
     )(pinned(x_a), pinned(x_b), pinned(acc))
     c_a, c_b = swap_both(corner_a, corner_b, "gy")
-    perm, field_a, field_b, coef, acc = pl.pallas_call(
-        strip_kernel,
-        out_shape=(in_vmem(*PLAIN), in_vmem(*FIELD), in_vmem(*FIELD), in_vmem(*COEF), in_vmem(64, LANES)),
-        in_specs=[VMEM_SPEC] * 9,
-        out_specs=(VMEM_SPEC,) * 5,
-        input_output_aliases={4: 0, 5: 1, 6: 2, 7: 3, 8: 4},
-        compiler_params=params(4),
-        cost_estimate=pl.CostEstimate(flops=10 * MIB, bytes_accessed=8 * MIB, transcendentals=0),
-        name="strip_stage",
-    )(*[pinned(a) for a in (x_a, x_b, y_a, y_b, perm, field_a, field_b, coef, acc)])
+    state = (perm, field_a, field_b, coef, acc)
+    for kernel, halos in ((x_strip_kernel, (x_a, x_b)), (y_strip_kernel, (y_a, y_b))):
+        state = pl.pallas_call(
+            kernel,
+            out_shape=(in_vmem(*PLAIN), in_vmem(*FIELD), in_vmem(*FIELD), in_vmem(*COEF), in_vmem(64, LANES)),
+            in_specs=[VMEM_SPEC] * 7,
+            out_specs=(VMEM_SPEC,) * 5,
+            input_output_aliases={2 + n: n for n in range(5)},
+            compiler_params=params(4),
+            cost_estimate=pl.CostEstimate(flops=10 * MIB, bytes_accessed=8 * MIB, transcendentals=0),
+            name=kernel.__name__,
+        )(*[pinned(a) for a in (*halos, *state)])
     rows, _, _, field_b, _ = pl.pallas_call(
         last_kernel,
         out_shape=(in_vmem(8, LANES), in_vmem(*PLAIN), in_vmem(*FIELD), in_vmem(*FIELD), in_vmem(*COEF)),
@@ -584,7 +597,7 @@
         input_output_aliases={2: 1, 3: 2, 4: 3, 5: 4},
         compiler_params=params(4),
         name="corner_stage",
-    )(*[pinned(a) for a in (c_a, c_b, perm, field_a, field_b, coef, acc)])
+    )(*[pinned(a) for a in (c_a, c_b, *state)])
     from_x = ahead(rows, 1, 0)
     from_y = ahead(rows, 0, 1)
     from_xy = ahead(rows, 1, 1)

time: 35.2 us -> 34.9 us (level)
  waiting for transfers between devices: 1.55 us -> 0.02 us
  starting transfers between devices: 21.6 us -> 22.7 us
    ppermute x3, waiting for transfers between devices: 1.54 us -> 0.01 us  [swap_both(): lax.ppermute(second, axis, swap_pairs(axis, 1 - FIRST_PAIRS[axis]))]
    ppermute x3, starting transfers between devices: 7.71 us -> 8.83 us  [ahead(): return lax.ppermute(array, ('gx', 'gy'), pairs)]
    pallas_call x1 -> x2, Pallas kernels: 3.31 us -> 3.33 us  [shards(): pl.pallas_call(kernel, out_shape=(in_vmem(*PLAIN), in_vmem(*FIELD), in_vm...]
  transfers between devices with their start and end apart: 9 -> 9, of which waited for: 1 -> 0; matrix products, arithmetic and copies ran while one was open for 0% -> 0% of each run, Pallas kernels for 21% -> 21%
where the time goes in v5:
time: 34.9 us; the launch traced here: 34.6 us
  starting transfers between devices  22.7 us (65%)
  Pallas kernels  10.4 us (30%)
  between operations  0.8 us (2%)
  other arithmetic  0.67 us (2%)
    ppermute x3, starting transfers between devices, swap_both(): lax.ppermute(second, axis, swap_pairs(axis, 1 - FIRST_PAIRS[axis]))  10.8 us
    ppermute x3, starting transfers between devices, ahead(): return lax.ppermute(array, ('gx', 'gy'), pairs)  8.83 us
    pallas_call x2, Pallas kernels, shards(): pl.pallas_call(kernel, out_shape=(in_vmem(*PLAIN), in_vmem(*FIELD), in_vm...  3.33 us
    ppermute x3, starting transfers between devices, swap_both(): lax.ppermute(first, axis, swap_pairs(axis, FIRST_PAIRS[axis]))  3.1 us
    pallas_call x1, Pallas kernels, shards(): pl.pallas_call(inner_kernel, out_shape=(in_vmem(*FIELD), in_vmem(*FIELD),...  2.1 us
    pallas_call x1, Pallas kernels, shards(): pl.pallas_call(x_face_kernel, out_shape=(in_vmem(*FIELD), in_vmem(*PLAIN)...  1.56 us
    pallas_call x1, Pallas kernels, shards(): pl.pallas_call(last_kernel, out_shape=(in_vmem(8, LANES), in_vmem(*PLAIN)...  1.56 us
    pallas_call x1, Pallas kernels, shards(): pl.pallas_call(basis_kernel, out_shape=jax.ShapeDtypeStruct((SLOTS, CB, C...  1.4 us
  transfers between devices with their start and end apart: 9, of which 0 were waited for; matrix products, arithmetic and copies ran while one was open for 0% of the time, Pallas kernels for 21%

profile of v5, /device:TPU:1, one launch (start us, length us, event | category | flops | bytes accessed | tf_op | source)
XLA Modules:
  0.0 34.6 jit_solution(8945351070603903263)
XLA Ops:
  0.6 1.6 %x_faces.1 = (f32[4624,128]{1,0:T(8,128)S(1)}, f32[592,128]{1,0:T(8,128)S(1)}, f32[576,128]{1,0:T(8,128)S(1)}, f32[576,128]{1,0:T(8,128)S(1)}, f32[2,8,4,16,128]...) custom-call(f32[8,16,16,128]{3,2,1,0:T(8,128)} %basis_hbm.1, s32[16,16,128]{2,1,0:T(8,128)} %labels_hbm.1, ...), custom_call_target="tpu_custom_call" | custom-call | tf_op jit(solution)/shard_map/x_faces/pallas_call | solution.py:535
  2.2 0.7 %collective-permute-start = (f32[576,128]{1,0:T(8,128)S(1)}, f32[576,128]{1,0:T(8,128)S(1)}, u32[]{:S(2)}, u32[]{:S(2)}) collective-permute-start(f32[576,128]{1,0:T(8,128)S(1)} %get-tuple-element.29), channel_id=1, source_target_pairs={{8,16},{16,8},{9,17},{17,9},{10,18},{18,10},{11,19},{19,11},{12,20... | collective-permute-start | bytes 884744 | tf_op jit(solution)/shard_map/ppermute | solution.py:510
  2.9 4.7 %collective-permute-start.1 = (f32[576,128]{1,0:T(8,128)S(1)}, f32[576,128]{1,0:T(8,128)S(1)}, u32[]{:S(2)}, u32[]{:S(2)}) collective-permute-start(f32[576,128]{1,0:T(8,128)S(1)} %get-tuple-element.30), channel_id=1, source_target_pairs={{0,8},{8,0},{16,24},{24,16},{1,9},{9,1},{17,25},{25,17},{2,10},{10... | collective-permute-start | bytes 884744 | tf_op jit(solution)/shard_map/ppermute | solution.py:511
  7.6 0.4 %y_faces.1 = (f32[4624,128]{1,0:T(8,128)S(1)}, f32[576,128]{1,0:T(8,128)S(1)}, f32[576,128]{1,0:T(8,128)S(1)}) custom-call(f32[4624,128]{1,0:T(8,128)S(1)} %get-tuple-element.31.field_in, f32[592,128]{1,0:T(8,128)S(1)} %get-tuple-element.32.perm.refs_2_, f32[2,8,4,16,128]{4,3,2,1,0:T(8,128)S(1)} %get-tuple-element.33.middle, ...), custom_call_target="tpu_custom_call", output_to_operand_aliasing={{0}: (0, {})} | custom-call | tf_op jit(solution)/shard_map/y_faces/pallas_call | solution.py:550
  8.0 1.3 %collective-permute-start.4 = (f32[576,128]{1,0:T(8,128)S(1)}, f32[576,128]{1,0:T(8,128)S(1)}, u32[]{:S(2)}, u32[]{:S(2)}) collective-permute-start(f32[576,128]{1,0:T(8,128)S(1)} %get-tuple-element.39), channel_id=1, source_target_pairs={{0,1},{1,0},{2,3},{3,2},{4,5},{5,4},{6,7},{7,6},{8,9},{9,8},{10,11... | collective-permute-start | bytes 884744 | tf_op jit(solution)/shard_map/ppermute | solution.py:510
  9.3 3.0 %collective-permute-start.5 = (f32[576,128]{1,0:T(8,128)S(1)}, f32[576,128]{1,0:T(8,128)S(1)}, u32[]{:S(2)}, u32[]{:S(2)}) collective-permute-start(f32[576,128]{1,0:T(8,128)S(1)} %get-tuple-element.40), channel_id=1, source_target_pairs={{1,2},{2,1},{3,4},{4,3},{5,6},{6,5},{9,10},{10,9},{11,12},{12,11},... | collective-permute-start | bytes 884744 | tf_op jit(solution)/shard_map/ppermute | solution.py:511
  12.4 2.1 %inner_stage.1 = (f32[4624,128]{1,0:T(8,128)S(1)}, f32[4624,128]{1,0:T(8,128)S(1)}, f32[7,592,128]{2,1,0:T(8,128)S(1)}, f32[64,128]{1,0:T(8,128)S(1)}) custom-call(f32[4624,128]{1,0:T(8,128)S(1)} %get-tuple-element.35.field_in, f32[592,128]{1,0:T(8,128)S(1)} %get-tuple-element.32.perm.refs_2_), custom_call_target="tpu_custom_call", output_to_operand_aliasing={{0}: (0, {})} | custom-call | flops 10485760 | bytes 8388608 | tf_op jit(solution)/shard_map/inner_stage/pallas_call | solution.py:560
  14.5 0.0 collective-permute-done.from_a.refs_0_
  14.5 0.0 collective-permute-done.1.from_b.refs_1_
  14.5 1.1 %collective-permute-start.2 = (f32[112,128]{1,0:T(8,128)S(1)}, f32[112,128]{1,0:T(8,128)S(1)}, u32[]{:S(2)}, u32[]{:S(2)}) collective-permute-start(f32[112,128]{1,0:T(8,128)S(1)} %get-tuple-element.37), channel_id=1, source_target_pairs={{0,1},{1,0},{2,3},{3,2},{4,5},{5,4},{6,7},{7,6},{8,9},{9,8},{10,11... | collective-permute-start | bytes 172040 | tf_op jit(solution)/shard_map/ppermute | solution.py:510
  15.7 3.0 %collective-permute-start.3 = (f32[112,128]{1,0:T(8,128)S(1)}, f32[112,128]{1,0:T(8,128)S(1)}, u32[]{:S(2)}, u32[]{:S(2)}) collective-permute-start(f32[112,128]{1,0:T(8,128)S(1)} %get-tuple-element.38), channel_id=1, source_target_pairs={{1,2},{2,1},{3,4},{4,3},{5,6},{6,5},{9,10},{10,9},{11,12},{12,11},... | collective-permute-start | bytes 172040 | tf_op jit(solution)/shard_map/ppermute | solution.py:511
  18.7 1.6 %x_strip_kernel.1 = (f32[592,128]{1,0:T(8,128)S(1)}, f32[4624,128]{1,0:T(8,128)S(1)}, f32[4624,128]{1,0:T(8,128)S(1)}, f32[7,592,128]{2,1,0:T(8,128)S(1)}, f32[64,128]{1,0:T(8,128)S(1)}) custom-call(f32[576,128]{1,0:T(8,128)S(1)} %collective-permute-done.from_a.refs_0_, ...), custom_call_target="tpu_custom_call", output_to_operand_aliasing={{0}: (2, {}), {1}: (3, {}), {2}: (4, {}), {3}: (5, {}), {4}... | custom-call | flops 10485760 | bytes 8388608 | tf_op jit(solution)/shard_map/x_strip_kernel/pallas_call | solution.py:582
  20.3 0.0 collective-permute-done.4.refs_0_
  20.3 0.0 collective-permute-done.5.refs_1_
  20.3 1.8 %y_strip_kernel.1 = (f32[592,128]{1,0:T(8,128)S(1)}, f32[4624,128]{1,0:T(8,128)S(1)}, f32[4624,128]{1,0:T(8,128)S(1)}, f32[7,592,128]{2,1,0:T(8,128)S(1)}, f32[64,128]{1,0:T(8,128)S(1)}) custom-call(f32[576,128]{1,0:T(8,128)S(1)} %collective-permute-done.4.refs_0_, ...), custom_call_target="tpu_custom_call", output_to_operand_aliasing={{0}: (2, {}), {1}: (3, {}), {2}: (4, {}), {3}: (5, {}), {4}... | custom-call | flops 10485760 | bytes 8388608 | tf_op jit(solution)/shard_map/y_strip_kernel/pallas_call | solution.py:582
  22.0 0.0 collective-permute-done.2.refs_0_
  22.1 0.0 collective-permute-done.3.refs_1_
  22.1 1.6 %corner_stage.1 = (f32[8,128]{1,0:T(8,128)S(1)}, f32[592,128]{1,0:T(8,128)S(1)}, f32[4624,128]{1,0:T(8,128)S(1)}, f32[4624,128]{1,0:T(8,128)S(1)}, f32[7,592,128]{2,1,0:T(8,128)S(1)}) custom-call(f32[112,128]{1,0:T(8,128)S(1)} %collective-permute-done.2.refs_0_, ...), custom_call_target="tpu_custom_call", output_to_operand_aliasing={{1}: (2, {}), {2}: (3, {}), {3}: (4, {}), {4}: (5, {})} | custom-call | tf_op jit(solution)/shard_map/corner_stage/pallas_call | solution.py:592
  23.6 3.7 %collective-permute-start.8 = (f32[8,128]{1,0:T(8,128)S(1)}, f32[8,128]{1,0:T(8,128)S(1)}, u32[]{:S(2)}, u32[]{:S(2)}) collective-permute-start(f32[8,128]{1,0:T(8,128)S(1)} %get-tuple-element.55), channel_id=1, source_target_pairs={{0,9},{1,10},{2,11},{3,12},{4,13},{5,14},{6,15},{8,17},{9,18},{10,... | collective-permute-start | bytes 12296 | tf_op jit(solution)/shard_map/ppermute | solution.py:522
  27.3 3.1 %collective-permute-start.7 = (f32[8,128]{1,0:T(8,128)S(1)}, f32[8,128]{1,0:T(8,128)S(1)}, u32[]{:S(2)}, u32[]{:S(2)}) collective-permute-start(f32[8,128]{1,0:T(8,128)S(1)} %get-tuple-element.55), channel_id=1, source_target_pairs={{0,1},{1,2},{2,3},{3,4},{4,5},{5,6},{6,7},{8,9},{9,10},{10,11},{11... | collective-permute-start | bytes 12296 | tf_op jit(solution)/shard_map/ppermute | solution.py:522
  30.4 2.1 %collective-permute-start.6 = (f32[8,128]{1,0:T(8,128)S(1)}, f32[8,128]{1,0:T(8,128)S(1)}, u32[]{:S(2)}, u32[]{:S(2)}) collective-permute-start(f32[8,128]{1,0:T(8,128)S(1)} %get-tuple-element.55), channel_id=1, source_target_pairs={{0,8},{1,9},{2,10},{3,11},{4,12},{5,13},{6,14},{7,15},{8,16},{9,17... | collective-permute-start | bytes 12296 | tf_op jit(solution)/shard_map/ppermute | solution.py:522
  32.5 1.4 %basis_out.1 = f32[8,16,16,128]{3,2,1,0:T(8,128)} custom-call(f32[4624,128]{1,0:T(8,128)S(1)} %get-tuple-element.54.field), custom_call_target="tpu_custom_call" | custom-call | bytes 2097152 | tf_op jit(solution)/shard_map/basis_out/pallas_call | solution.py:604
  33.9 0.0 collective-permute-done.8
  33.9 0.7 %add_bitcast_fusion = f32[27,1,1,8]{0,3,2,1:T(8,128)} fusion(f32[8,128]{1,0:T(8,128)S(1)} %collective-permute-done.8, f32[8,128]{1,0:T(8,128)S(1)} %collective-permute-done.7, f32[8,128]{1,0:T(8,128)S(1)} %collective-permute-done.6, f32[8,128]{1,0:T(8,128)S(1)} %get-tuple-element.55), kind=kLoop, calls=%fused_computation | loop fusion | flops 648 | bytes 4320 | tf_op jit(solution)/shard_map/reshape | solution.py:618
  (3 shorter events, 0.0 us)
Async XLA Ops:
  2.2 12.3 %collective-permute-start = (f32[576,128]{1,0:T(8,128)S(1)}, f32[576,128]{1,0:T(8,128)S(1)}, u32[]{:S(2)}, u32[]{:S(2)}) collective-permute-start(f32[576,128]{1,0:T(8,128)S(1)} %get-tuple-element.29), channel_id=1, source_target_pairs={{8,16},{16,8},{9,17},{17,9},{10,18},{18,10},{11,19},{19,11},{12,20... | collective-permute-start | bytes 884744 | tf_op jit(solution)/shard_map/ppermute | solution.py:510
  2.9 11.6 %collective-permute-start.1 = (f32[576,128]{1,0:T(8,128)S(1)}, f32[576,128]{1,0:T(8,128)S(1)}, u32[]{:S(2)}, u32[]{:S(2)}) collective-permute-start(f32[576,128]{1,0:T(8,128)S(1)} %get-tuple-element.30), channel_id=1, source_target_pairs={{0,8},{8,0},{16,24},{24,16},{1,9},{9,1},{17,25},{25,17},{2,10},{10... | collective-permute-start | bytes 884744 | tf_op jit(solution)/shard_map/ppermute | solution.py:511
  8.0 12.2 %collective-permute-start.4 = (f32[576,128]{1,0:T(8,128)S(1)}, f32[576,128]{1,0:T(8,128)S(1)}, u32[]{:S(2)}, u32[]{:S(2)}) collective-permute-start(f32[576,128]{1,0:T(8,128)S(1)} %get-tuple-element.39), channel_id=1, source_target_pairs={{0,1},{1,0},{2,3},{3,2},{4,5},{5,4},{6,7},{7,6},{8,9},{9,8},{10,11... | collective-permute-start | bytes 884744 | tf_op jit(solution)/shard_map/ppermute | solution.py:510
  9.3 10.9 %collective-permute-start.5 = (f32[576,128]{1,0:T(8,128)S(1)}, f32[576,128]{1,0:T(8,128)S(1)}, u32[]{:S(2)}, u32[]{:S(2)}) collective-permute-start(f32[576,128]{1,0:T(8,128)S(1)} %get-tuple-element.40), channel_id=1, source_target_pairs={{1,2},{2,1},{3,4},{4,3},{5,6},{6,5},{9,10},{10,9},{11,12},{12,11},... | collective-permute-start | bytes 884744 | tf_op jit(solution)/shard_map/ppermute | solution.py:511
  14.5 7.5 %collective-permute-start.2 = (f32[112,128]{1,0:T(8,128)S(1)}, f32[112,128]{1,0:T(8,128)S(1)}, u32[]{:S(2)}, u32[]{:S(2)}) collective-permute-start(f32[112,128]{1,0:T(8,128)S(1)} %get-tuple-element.37), channel_id=1, source_target_pairs={{0,1},{1,0},{2,3},{3,2},{4,5},{5,4},{6,7},{7,6},{8,9},{9,8},{10,11... | collective-permute-start | bytes 172040 | tf_op jit(solution)/shard_map/ppermute | solution.py:510
  15.7 6.4 %collective-permute-start.3 = (f32[112,128]{1,0:T(8,128)S(1)}, f32[112,128]{1,0:T(8,128)S(1)}, u32[]{:S(2)}, u32[]{:S(2)}) collective-permute-start(f32[112,128]{1,0:T(8,128)S(1)} %get-tuple-element.38), channel_id=1, source_target_pairs={{1,2},{2,1},{3,4},{4,3},{5,6},{6,5},{9,10},{10,9},{11,12},{12,11},... | collective-permute-start | bytes 172040 | tf_op jit(solution)/shard_map/ppermute | solution.py:511
  23.6 10.3 %collective-permute-start.8 = (f32[8,128]{1,0:T(8,128)S(1)}, f32[8,128]{1,0:T(8,128)S(1)}, u32[]{:S(2)}, u32[]{:S(2)}) collective-permute-start(f32[8,128]{1,0:T(8,128)S(1)} %get-tuple-element.55), channel_id=1, source_target_pairs={{0,9},{1,10},{2,11},{3,12},{4,13},{5,14},{6,15},{8,17},{9,18},{10,... | collective-permute-start | bytes 12296 | tf_op jit(solution)/shard_map/ppermute | solution.py:522
  27.3 6.6 %collective-permute-start.7 = (f32[8,128]{1,0:T(8,128)S(1)}, f32[8,128]{1,0:T(8,128)S(1)}, u32[]{:S(2)}, u32[]{:S(2)}) collective-permute-start(f32[8,128]{1,0:T(8,128)S(1)} %get-tuple-element.55), channel_id=1, source_target_pairs={{0,1},{1,2},{2,3},{3,4},{4,5},{5,6},{6,7},{8,9},{9,10},{10,11},{11... | collective-permute-start | bytes 12296 | tf_op jit(solution)/shard_map/ppermute | solution.py:522
  30.4 3.5 %collective-permute-start.6 = (f32[8,128]{1,0:T(8,128)S(1)}, f32[8,128]{1,0:T(8,128)S(1)}, u32[]{:S(2)}, u32[]{:S(2)}) collective-permute-start(f32[8,128]{1,0:T(8,128)S(1)} %get-tuple-element.55), channel_id=1, source_target_pairs={{0,8},{1,9},{2,10},{3,11},{4,12},{5,13},{6,14},{7,15},{8,16},{9,17... | collective-permute-start | bytes 12296 | tf_op jit(solution)/shard_map/ppermute | solution.py:522
